TPU v7x, 128 devices: a whole 4x4x4 slice. The times are simulated.
128 devices in a mesh: adapter: 16 (over y, z), tensor: 8 (over x, core).
Axes of the slice: x: 4, y: 4, z: 4, core: 2. Of those that a mesh axis runs over, the one named last changes fastest.
Arguments:
- tokens: bfloat16 [1024, 8192], P('adapter', 'tensor'), may hold values from -6 to 6
- token_adapter: int32 [1024], P('adapter'), may hold values from 0 to 31, as said below
- adapter_slot_table: int32 [32], replicated, may hold values from 0 to 31, each once
- gate_matrix: bfloat16 [8192, 28672], P(None, ('adapter', 'tensor')), may hold values from -0.0625 to 0.0625
- up_matrix: bfloat16 [8192, 28672], P(None, ('adapter', 'tensor')), may hold values from -0.0625 to 0.0625
- down_matrix: bfloat16 [28672, 8192], P(('adapter', 'tensor')), may hold values from -0.03125 to 0.03125
- adapter_entry_maps: bfloat16 [32, 8192, 128], P('adapter'), may hold values from -0.0625 to 0.0625
- adapter_gate_exit: bfloat16 [32, 64, 28672], P(None, None, ('adapter', 'tensor')), may hold values from -0.375 to 0.375
- adapter_up_exit: bfloat16 [32, 64, 28672], P(None, None, ('adapter', 'tensor')), may hold values from -0.375 to 0.375
- adapter_down_entry: bfloat16 [32, 28672, 64], P(None, ('adapter', 'tensor')), may hold values from -0.03125 to 0.03125
- adapter_down_exit: bfloat16 [32, 64, 8192], P('adapter', None, 'tensor'), may hold values from -0.375 to 0.375
Outputs:
- mixed: bfloat16 [1024, 8192], P('adapter', 'tensor')
Inputs may be any that keep to these rules, and one draw needn't show every extreme that they name: `token_adapter`: every adapter is the adapter of 1 to 80 tokens, and some adapter of exactly 80. `adapter_slot_table`: each slot number appears once.
All inputs are finite; a program needn't handle non-finite values.
Results may differ from a plain program's by a relative error of at most 0.0055.
Values may be sent and summed in bfloat16 or wider, within the bound.
No kernel may reach another device: no remote copies, remote signals or barrier semaphores. Data moves between devices by JAX's collectives and lax.ppermute only.
A program may use at most 192 MiB of HBM per device.

v0:
```python
import jax
import jax.numpy as jnp
from jax import lax
from jax.sharding import PartitionSpec as P

SEGMENT_TOKENS = 80


def token_layout(token_adapter, adapter_slot_table, seg_rows):
    token_count = token_adapter.shape[0]
    adapter_count = adapter_slot_table.shape[0]
    member = (token_adapter[:, None] == jnp.arange(adapter_count, dtype=jnp.int32)[None, :]).astype(
        jnp.int32
    )
    earlier = jnp.cumsum(member, axis=0) - member
    rank_in = jnp.sum(earlier * member, axis=1)
    slot_index = jnp.sum(member * adapter_slot_table[None, :], axis=1)
    slot_row = slot_index * seg_rows + rank_in
    token_of_row = jnp.full((adapter_count * seg_rows,), token_count, jnp.int32)
    token_of_row = token_of_row.at[slot_row].set(jnp.arange(token_count, dtype=jnp.int32))
    return (slot_row, token_of_row)


def on_device(
    tokens,
    token_adapter,
    adapter_slot_table,
    gate_matrix,
    up_matrix,
    down_matrix,
    adapter_entry_maps,
    adapter_gate_exit,
    adapter_up_exit,
    adapter_down_entry,
    adapter_down_exit,
):
    home_rows = lax.all_gather(tokens, "tensor", axis=1, tiled=True)
    every_rows, every_ids = (
        lax.all_gather(home_rows, "adapter", axis=0, tiled=True),
        lax.all_gather(token_adapter, "adapter", axis=0, tiled=True),
    )
    token_count = every_rows.shape[0]
    local_tokens = home_rows.shape[0]
    adapter_count = adapter_slot_table.shape[0]
    kept_slots = adapter_entry_maps.shape[0]
    rank_span = adapter_gate_exit.shape[1]
    slot_row, token_of_row = token_layout(every_ids, adapter_slot_table, SEGMENT_TOKENS)
    is_filled = token_of_row < token_count
    safe_index = jnp.minimum(token_of_row, token_count - 1)
    owner_index = lax.axis_index("adapter")
    own_tokens = lax.dynamic_slice_in_dim(
        token_of_row, owner_index * kept_slots * SEGMENT_TOKENS, kept_slots * SEGMENT_TOKENS
    )
    own_filled = own_tokens < token_count
    local_rows = jnp.where(
        own_filled[:, None], every_rows[jnp.minimum(own_tokens, token_count - 1)], 0
    )
    local_rows = local_rows.reshape(kept_slots, SEGMENT_TOKENS, every_rows.shape[1])
    low_own = jnp.einsum(
        "ace,aeg->acg", local_rows, adapter_entry_maps, preferred_element_type=jnp.float32
    ).astype(jnp.bfloat16)
    reduced_gathered = lax.all_gather(
        low_own.reshape(kept_slots * SEGMENT_TOKENS, 2 * rank_span), "adapter", axis=0, tiled=True
    )
    reduced_gathered = reduced_gathered.reshape(adapter_count, SEGMENT_TOKENS, 2 * rank_span)
    gate_correction = jnp.einsum(
        "mdq,mqn->mdn",
        reduced_gathered[..., :rank_span],
        adapter_gate_exit,
        preferred_element_type=jnp.float32,
    )
    up_correction = jnp.einsum(
        "mdq,mqn->mdn",
        reduced_gathered[..., rank_span:],
        adapter_up_exit,
        preferred_element_type=jnp.float32,
    )
    gate_sum = (
        jnp.dot(every_rows, gate_matrix, preferred_element_type=jnp.float32)
        + gate_correction.reshape(adapter_count * SEGMENT_TOKENS, -1)[slot_row]
    )
    up_sum = (
        jnp.dot(every_rows, up_matrix, preferred_element_type=jnp.float32)
        + up_correction.reshape(adapter_count * SEGMENT_TOKENS, -1)[slot_row]
    )
    hidden = (jax.nn.silu(gate_sum) * up_sum).astype(jnp.bfloat16)
    hidden_padded = jnp.where(is_filled[:, None], hidden[safe_index], 0).reshape(
        adapter_count, SEGMENT_TOKENS, hidden.shape[1]
    )
    down_part = jnp.einsum(
        "uvm,umj->uvj", hidden_padded, adapter_down_entry, preferred_element_type=jnp.float32
    )
    down_total = lax.psum(down_part, ("adapter", "tensor"))
    local_reduced = lax.dynamic_slice_in_dim(
        down_total, owner_index * kept_slots, kept_slots, 0
    ).astype(jnp.bfloat16)
    own_delta = jnp.einsum(
        "uhz,uza->uha", local_reduced, adapter_down_exit, preferred_element_type=jnp.float32
    )
    column_span = adapter_down_exit.shape[2]
    own_delta = own_delta.reshape(kept_slots * SEGMENT_TOKENS, column_span)
    product = jnp.dot(hidden, down_matrix, preferred_element_type=jnp.float32)
    summed = lax.psum_scatter(product, "adapter", scatter_dimension=0, tiled=True)
    summed = lax.psum_scatter(summed, "tensor", scatter_dimension=1, tiled=True)
    every_delta = lax.all_gather(own_delta, "adapter", axis=0, tiled=True)
    home_slot_rows = lax.dynamic_slice_in_dim(slot_row, owner_index * local_tokens, local_tokens)
    summed = summed + every_delta[home_slot_rows]
    return summed.astype(jnp.bfloat16)


def solution(mesh):
    return jax.shard_map(
        on_device,
        mesh=mesh,
        in_specs=(
            P("adapter", "tensor"),
            P("adapter"),
            P(),
            P(None, ("adapter", "tensor")),
            P(None, ("adapter", "tensor")),
            P(("adapter", "tensor"), None),
            P("adapter", None, None),
            P(None, None, ("adapter", "tensor")),
            P(None, None, ("adapter", "tensor")),
            P(None, ("adapter", "tensor"), None),
            P("adapter", None, "tensor"),
        ),
        out_specs=P("adapter", "tensor"),
        check_vma=False,
    )
```

profile of v0, /device:TPU:0, one launch (start us, length us, event | category | flops | bytes accessed | tf_op | source)
XLA Modules:
  0.0 563.2 jit_solution(4052931335230623822)
XLA Ops:
  6.5 0.7 all-gather.4.cloned.1.call-update
  7.3 27.6 %all-gather.4.cloned.1.call-done = bf16[64,8192]{1,0:T(8,128)(2,1)} async-done(((bf16[64,1024]{1,0:T(8,128)(2,1)}), bf16[64,8192]{1,0:T(8,128)(2,1)}) %all-gather.4.cloned.1.call-update) | async-done | bytes 1048592 | tf_op jit(solution)/shard_map/all_gather | solution.py:37
  35.0 1.2 dynamic-slice
  36.9 0.9 dynamic-update-slice
  37.7 16.5 %all-reduce = s32[1024]{0:T(1024)S(1)} all-reduce(s32[1024]{0:T(1024)S(1)} %dynamic-update-slice), channel_id=1, replica_groups=mesh['adapter'=16,'tensor'=8] {'adapter'}, use_global_device_ids=true, to_apply=%add | all-reduce | flops 1024 | bytes 8192
  54.2 9.0 %reduce-window.6 = s32[32,8,128]{2,1,0:T(8,128)S(1)} reduce-window(s32[32,8,128]{2,1,0:T(8,128)S(1)} %fusion.20, s32[]{:T(128)} %constant.14.clone.1), window={size=1x1x128 pad=0_0x0_0x127_0}, to_apply=%region_1.2 | reduce-window | flops 4161536 | bytes 262148 | tf_op jit(solution)/shard_map/reduce-window
  63.7 0.7 select_reduce_fusion
  64.5 0.6 copy-done.5
  65.1 4.3 scatter_custom_fusion
  69.7 78.7 %all-gather.6.cloned.1.call-done = bf16[1024,8192]{1,0:T(8,128)(2,1)} async-done(((bf16[64,8192]{1,0:T(8,128)(2,1)}), bf16[1024,8192]{1,0:T(8,128)(2,1)}) %all-gather.6.cloned.1.call-update) | async-done | bytes 16777232 | tf_op jit(solution)/shard_map/all_gather | solution.py:39
  148.4 14.0 %gather_fusion = bf16[160,8192]{1,0:T(8,128)(2,1)} fusion(bf16[1024,8192]{1,0:T(8,128)(2,1)} %all-gather.6.cloned.1.call-done, s32[1024]{0:T(1024)S(1)} %pad_clamp_fusion.2), kind=kCustom, calls=%fused_computation | custom fusion | bytes 5243520 | tf_op jit(solution)/shard_map/gather | solution.py:56
  162.4 4.0 fusion.9
  166.4 24.0 %all_gather.18 = bf16[2560,128]{1,0:T(8,128)(2,1)S(1)} all-gather(bf16[160,128]{1,0:T(8,128)(2,1)S(1)} %bitcast.49), channel_id=1, replica_groups=mesh['adapter'=16,'tensor'=8] {'adapter'}, dimensions={0}, use_global_device_ids=true | all-gather | bytes 696320 | tf_op jit(solution)/shard_map/all_gather | solution.py:62
  190.4 2.0 fusion.14
  192.4 5.2 gather_fusion.1
  197.6 1.3 copy.18
  198.9 1.8 fusion.12
  200.7 4.7 gather_fusion.2
  205.4 1.5 copy.20
  206.9 10.0 %convolution_add_fusion.1 = f32[1024,224]{0,1:T(8,128)S(1)} fusion(f32[1024,224]{0,1:T(8,128)S(1)} %copy-done.3, bf16[1024,8192]{1,0:T(8,128)(2,1)} %all-gather.6.cloned.1.call-done, bf16[8192,224]{0,1:T(8,128)(2,1)} %param.14), kind=kOutput, calls=%fused_computation.15 | convolution fusion | flops 3758325760 | bytes 22282240 | tf_op jit(solution)/shard_map/dot_general | solution.py:79
  216.9 9.0 %fusion.8 = bf16[1024,224]{0,1:T(8,128)(2,1)S(1)} fusion(f32[1024,224]{0,1:T(8,128)S(1)} %copy.20, bf16[1024,8192]{1,0:T(8,128)(2,1)} %all-gather.6.cloned.1.call-done, bf16[8192,224]{0,1:T(8,128)(2,1)S(1)} %copy-done.6, f32[1024,224]{0,1:T(8,128)S(1)} %convolution_add_fusion.1), kind=kOutput, calls=%fused_computation.16 | convolution fusion | flops 3759702016 | bytes 22740992 | tf_op jit(solution)/shard_map/dot_general | solution.py:83
  226.0 13.1 %fusion.27 = f32[1024,8192]{1,0:T(8,128)} fusion(bf16[1024,224]{0,1:T(8,128)(2,1)S(1)} %fusion.8, bf16[224,8192]{1,0:T(8,128)(2,1)S(1)} %copy-done.2), kind=kOutput, calls=%fused_computation.51 | convolution fusion | flops 3758096384 | bytes 37683200 | tf_op jit(solution)/shard_map/dot_general | solution.py:102
  239.5 7.6 %gather_fusion.3 = bf16[2560,224]{1,0:T(8,128)(2,1)S(1)} fusion(bf16[1024,224]{1,0:T(8,128)(2,1)S(1)} %copy.21, s32[3072]{0:T(1024)S(1)} %pad_clamp_fusion), kind=kCustom, calls=%fused_computation.3 | custom fusion | bytes 2304000 | tf_op jit(solution)/shard_map/gather | solution.py:87
  247.1 2.0 fusion.3
  249.1 74.0 %all-reduce.2 = bf16[32,80,64]{1,2,0:T(8,128)(2,1)S(1)} all-reduce(f32[32,80,64]{1,2,0:T(8,128)S(1)} %fusion.3), channel_id=1, replica_groups=mesh['adapter'=16,'tensor'=8] {'adapter','tensor'}, use_global_device_ids=true, to_apply=%region_7.8 | all-reduce | flops 163840 | bytes 983040 | tf_op jit(solution)/shard_map/psum | solution.py:93
  323.1 1.1 fusion.21
  324.4 113.5 %reduce-scatter.3.cloned.1.call-done = f32[64,8192]{1,0:T(8,128)} async-done(((f32[1024,8192]{1,0:T(8,128)}), f32[64,8192]{1,0:T(8,128)}) %reduce-scatter.3.cloned.1.call-update) | async-done | bytes 2097168 | tf_op jit(solution)/shard_map/reduce_scatter | solution.py:103
  437.8 0.8 compare_select_fusion.3
  438.6 81.0 %all-gather.8.cloned.1.call-done = f32[2560,1024]{1,0:T(8,128)} async-done(((f32[160,1024]{1,0:T(8,128)}), f32[2560,1024]{1,0:T(8,128)}) %all-gather.8.cloned.1.call-update) | async-done | bytes 10485776 | tf_op jit(solution)/shard_map/all_gather | solution.py:105
  519.6 4.8 gather_fusion.4
  524.4 30.6 %reduce-scatter.5.cloned.1.call-done = f32[64,1024]{1,0:T(8,128)} async-done(((f32[64,8192]{1,0:T(8,128)}), f32[64,1024]{1,0:T(8,128)}) %reduce-scatter.5.cloned.1.call-update) | async-done | bytes 262160 | tf_op jit(solution)/shard_map/reduce_scatter | solution.py:104
  555.0 1.6 add_convert_fusion
  (44 shorter events, 1.3 us)
Async XLA Ops:
  6.5 183.9 %copy-start = (bf16[32,64,224]{2,1,0:T(8,128)(2,1)S(1)}, bf16[32,64,224]{2,1,0:T(8,128)(2,1)}, u32[]{:S(2)}) copy-start(bf16[32,64,224]{2,1,0:T(8,128)(2,1)} %param.18) | copy-start | bytes 2752516
  6.5 28.3 %all-gather.4.cloned.1.call-start = ((), (), s32[]{:S(2)}) async-start(), calls=%async_computation.2 | async-start | bytes 1179648 | tf_op jit(solution)/shard_map/all_gather | solution.py:37
  7.3 141.1 %all-gather.6.cloned.1.call-start = ((), (), s32[]{:S(2)}) async-start(), calls=%async_computation.3 | async-start | bytes 17825792 | tf_op jit(solution)/shard_map/all_gather | solution.py:39
  34.9 402.9 %reduce-scatter.3.cloned.1.call-start = ((), (), s32[]{:S(2)}) async-start(), calls=%async_computation.4 | async-start | bytes 35651584 | tf_op jit(solution)/shard_map/reduce_scatter | solution.py:103
  64.5 0.6 copy-start.5
  200.7 6.2 %copy-start.3 = (f32[1024,224]{0,1:T(8,128)S(1)}, f32[1024,224]{0,1:T(8,128)}, u32[]{:S(2)}) copy-start(f32[1024,224]{0,1:T(8,128)} %copy.18) | copy-start | bytes 2752516
  206.9 10.0 %copy-start.6 = (bf16[8192,224]{0,1:T(8,128)(2,1)S(1)}, bf16[8192,224]{0,1:T(8,128)(2,1)}, u32[]{:S(2)}) copy-start(bf16[8192,224]{0,1:T(8,128)(2,1)} %param.15) | copy-start | bytes 11010052
  216.9 9.1 %copy-start.2 = (bf16[224,8192]{1,0:T(8,128)(2,1)S(1)}, bf16[224,8192]{1,0:T(8,128)(2,1)}, u32[]{:S(2)}) copy-start(bf16[224,8192]{1,0:T(8,128)(2,1)} %param.16) | copy-start | bytes 11010052
  239.1 280.5 %all-gather.8.cloned.1.call-start = ((), (), s32[]{:S(2)}) async-start(), calls=%async_computation.6 | async-start | bytes 11141120 | tf_op jit(solution)/shard_map/all_gather | solution.py:105
  247.1 76.0 %copy-start.4 = (bf16[2,64,1024]{2,1,0:T(8,128)(2,1)S(1)}, bf16[2,64,1024]{2,1,0:T(8,128)(2,1)}, u32[]{:S(2)}) copy-start(bf16[2,64,1024]{2,1,0:T(8,128)(2,1)} %param.21) | copy-start | bytes 786436
  249.1 307.6 %copy-start.1 = (bf16[32,64,224]{2,1,0:T(8,128)(2,1)S(1)}, bf16[32,64,224]{2,1,0:T(8,128)(2,1)}, u32[]{:S(2)}) copy-start(bf16[32,64,224]{2,1,0:T(8,128)(2,1)} %param.18) | copy-start | bytes 2752516
  324.3 230.7 %reduce-scatter.5.cloned.1.call-start = ((), (), s32[]{:S(2)}) async-start(), calls=%async_computation.5 | async-start | bytes 2359296 | tf_op jit(solution)/shard_map/reduce_scatter | solution.py:104
Sparse Core Ops, SparseCore 0:
  9.1 25.7 all-gather.3
  37.0 111.3 all-gather.5
  239.3 198.5 reduce-scatter.2
  439.8 79.7 all-gather.7
  521.9 33.1 reduce-scatter.4
where the time goes:
time: 564 us; the launch traced here: 563 us
  waiting for transfers between devices  332 us (59%)
  blocking collectives  114 us (20%)
  local copies, waits for them, and re-layouts  46.7 us (8%)
  matrix products  43 us (8%)
  between operations  14.1 us (2%)
  other arithmetic  12.5 us (2%)
    reduce_scatter x1, waiting for transfers between devices, on_device(): lax.psum_scatter(product, 'adapter', scatter_dimension=0, tiled=True)  113 us
    all_gather x1, waiting for transfers between devices, on_device(): every_delta = lax.all_gather(own_delta, 'adapter', axis=0, tiled=True)  81 us
    all_gather x1, waiting for transfers between devices, on_device(): lax.all_gather(home_rows, 'adapter', axis=0, tiled=True)  78.7 us
    psum x1, blocking collectives, on_device(): down_total = lax.psum(down_part, ('adapter', 'tensor'))  74 us
    reduce_scatter x1, waiting for transfers between devices, on_device(): summed = lax.psum_scatter(summed, 'tensor', scatter_dimension=1, tiled=True)  30.6 us
    all_gather x1, waiting for transfers between devices, on_device(): home_rows = lax.all_gather(tokens, 'tensor', axis=1, tiled=True)  27.6 us
    all_gather x1, blocking collectives, on_device(): lax.all_gather(low_own.reshape(kept_slots * SEGMENT_TOKENS, 2 * rank_span...  24 us
    unnamed x1, blocking collectives  16.5 us
  transfers between devices with their start and end apart: 5, of which 5 were waited for; matrix products, arithmetic and copies ran while one was open for 6% of the time, Pallas kernels for 0%

commit v1 on v0

v1 whole, which is shorter than its diff:
```python
import functools

import jax
import jax.numpy as jnp
import numpy as np
from jax import lax
from jax.experimental import pallas as pl
from jax.experimental.pallas import tpu as pltpu
from jax.sharding import PartitionSpec as P

SEGMENT = 80
BF = jnp.bfloat16
F32 = jnp.float32
AXES = ("adapter", "tensor")
VMEM_LIMIT = 60 * 1024 * 1024


def pairs(move):
    out = []
    for i in range(128):
        y, z, x, c = i // 32, (i // 8) % 4, (i // 2) % 4, i % 2
        ty, tz, tx, tc = move(y, z, x, c)
        out.append((i, (ty % 4) * 32 + (tz % 4) * 8 + (tx % 4) * 2 + tc % 2))
    return out


def send(value, dy=0, dz=0, dx=0, dc=0):
    return lax.ppermute(value, AXES, pairs(lambda y, z, x, c: (y + dy, z + dz, x + dx, c + dc)))


def ring(value, axis):
    def move(y, z, x, c):
        d = 1 - 2 * c
        return (y + d, z, x, c) if axis == "y" else (y, z + d, x, c)

    return lax.ppermute(value, AXES, pairs(move))


def params(n=1):
    return pltpu.CompilerParams(
        dimension_semantics=("arbitrary",) * n, vmem_limit_bytes=VMEM_LIMIT
    )


def low_kernel(x_ref, e_ref, s_ref, o_ref, acc):
    k = pl.program_id(0)
    x = x_ref[...].reshape(1024, 1024)

    @pl.when(k == 0)
    def _():
        acc[...] = jnp.zeros_like(acc)

    for j in range(2):
        acc[j] += jnp.dot(x, e_ref[j], preferred_element_type=F32)

    @pl.when(k == pl.num_programs(0) - 1)
    def _():
        for j in range(2):
            o_ref[j] = jnp.dot(
                s_ref[j], acc[j].astype(BF), preferred_element_type=F32
            ).astype(BF)


def low_own_rows(every, entry, select):
    return pl.pallas_call(
        low_kernel,
        grid=(8,),
        in_specs=[
            pl.BlockSpec((16, 1, 64, 1024), lambda k: (0, k, 0, 0)),
            pl.BlockSpec((2, 1024, 128), lambda k: (0, k, 0)),
            pl.BlockSpec((2, SEGMENT, 1024), lambda k: (0, 0, 0)),
        ],
        out_specs=pl.BlockSpec((2, SEGMENT, 128), lambda k: (0, 0, 0)),
        out_shape=jax.ShapeDtypeStruct((2, SEGMENT, 128), BF),
        scratch_shapes=[pltpu.VMEM((2, 1024, 128), F32)],
        compiler_params=params(),
        cost_estimate=pl.CostEstimate(
            flops=2 * 1024 * 8192 * 256, bytes_accessed=21 << 20, transcendentals=0
        ),
        name="low_own",
    )(every, entry, select)


def gate_up_kernel(x_ref, g_ref, u_ref, go_ref, uo_ref):
    k = pl.program_id(0)
    x = x_ref[...].reshape(1024, 1024)

    @pl.when(k == 0)
    def _():
        go_ref[...] = jnp.zeros_like(go_ref)
        uo_ref[...] = jnp.zeros_like(uo_ref)

    go_ref[...] += jnp.dot(x, g_ref[...], preferred_element_type=F32)
    uo_ref[...] += jnp.dot(x, u_ref[...], preferred_element_type=F32)


def gate_up(every, gate, up):
    n = gate.shape[1]
    return pl.pallas_call(
        gate_up_kernel,
        grid=(8,),
        in_specs=[
            pl.BlockSpec((16, 1, 64, 1024), lambda k: (0, k, 0, 0)),
            pl.BlockSpec((1024, n), lambda k: (k, 0)),
            pl.BlockSpec((1024, n), lambda k: (k, 0)),
        ],
        out_specs=[pl.BlockSpec((1024, n), lambda k: (0, 0))] * 2,
        out_shape=[jax.ShapeDtypeStruct((1024, n), F32)] * 2,
        compiler_params=params(),
        cost_estimate=pl.CostEstimate(
            flops=2 * 1024 * 8192 * 512, bytes_accessed=25 << 20, transcendentals=0
        ),
        name="gate_up",
    )(every, gate, up)


def hidden_kernel(
    place, g_ref, u_ref, q_ref, m_ref, low_ref, ge_ref, ue_ref, de_ref, h_ref, d_ref
):
    low = jnp.dot(q_ref[...], low_ref[...], preferred_element_type=F32)
    lg = low[:, :64].astype(BF)
    lu = low[:, 64:].astype(BF)
    lg = jnp.concatenate([lg] * 4, axis=1)
    lu = jnp.concatenate([lu] * 4, axis=1)
    gate = g_ref[...]
    up = u_ref[...]
    for j in range(8):
        mask = m_ref[:, 256 * j : 256 * (j + 1)]
        gate += jnp.dot(lg * mask, ge_ref[pl.ds(256 * j, 256)], preferred_element_type=F32)
        up += jnp.dot(lu * mask, ue_ref[pl.ds(256 * j, 256)], preferred_element_type=F32)
    hidden = (gate / (1.0 + jnp.exp(-gate)) * up).astype(BF)
    down = jnp.zeros((256, 256), F32)
    for j in range(8):
        mask = m_ref[:, 256 * j : 256 * (j + 1)].astype(F32)
        down += jnp.dot(hidden, de_ref[j], preferred_element_type=F32) * mask
    down = down[:, :128] + down[:, 128:]
    for z in range(4):
        at = place[4 + z]
        h_ref[0, at] = hidden[64 * z : 64 * (z + 1)]
        d_ref[0, at] = down[64 * z : 64 * (z + 1)]


def hidden_rows(place, gate, up, pick, mask, low, gate_exit, up_exit, down_entry):
    n = gate.shape[1]
    return pl.pallas_call(
        hidden_kernel,
        grid_spec=pltpu.PrefetchScalarGridSpec(
            num_scalar_prefetch=1,
            grid=(4,),
            in_specs=[
                pl.BlockSpec((256, n), lambda i, p: (i, 0)),
                pl.BlockSpec((256, n), lambda i, p: (i, 0)),
                pl.BlockSpec((256, 2560), lambda i, p: (i, 0)),
                pl.BlockSpec((256, 2048), lambda i, p: (i, 0)),
                pl.BlockSpec((2560, 128), lambda i, p: (0, 0)),
                pl.BlockSpec((2048, n), lambda i, p: (0, 0)),
                pl.BlockSpec((2048, n), lambda i, p: (0, 0)),
                pl.BlockSpec((8, n, 256), lambda i, p: (0, 0, 0)),
            ],
            out_specs=[
                pl.BlockSpec((1, 4, 64, n), lambda i, p: (p[i], 0, 0, 0)),
                pl.BlockSpec((1, 4, 64, 128), lambda i, p: (p[i], 0, 0, 0)),
            ],
        ),
        out_shape=[
            jax.ShapeDtypeStruct((4, 4, 64, n), BF),
            jax.ShapeDtypeStruct((4, 4, 64, 128), F32),
        ],
        compiler_params=params(),
        cost_estimate=pl.CostEstimate(
            flops=2 * 1024 * 2560 * 512, bytes_accessed=16 << 20, transcendentals=1024 * n
        ),
        name="hidden_rows",
    )(place, gate, up, pick, mask, low, gate_exit, up_exit, down_entry)


def part_kernel(with_ring, with_extra, *refs):
    refs = list(refs)
    h_ref, w_ref, c_ref = refs[:3]
    o_ref = refs[-1]
    rest = refs[3:-1]
    r_ref = rest.pop(0) if with_ring else None
    n = w_ref.shape[1]
    for j in range(0, n, 1024):
        at = pl.ds(j, 1024)
        total = jnp.dot(h_ref[...], w_ref[:, at], preferred_element_type=F32)
        total += c_ref[:, at].astype(F32)
        if with_ring:
            total += r_ref[:, at].astype(F32)
        o_ref[:, at] = total.astype(o_ref.dtype)
    if with_extra:
        d_ref, e_ref = rest
        total = d_ref[...] + e_ref[...].astype(F32)
        if with_ring:
            total += r_ref[:, pl.ds(n, 128)].astype(F32)
        o_ref[:, pl.ds(n, 128)] = total.astype(o_ref.dtype)


def part(h, w, other, row, column, ringed, extra, dtype):
    rows, k = h.shape
    n = w.shape[1]
    args = [h, w, other]
    specs = [
        pl.BlockSpec((rows, k), lambda i: (0, 0)),
        pl.BlockSpec((k, n), lambda i: (0, 0)),
        pl.BlockSpec((rows, n), lambda i: (row, column)),
    ]
    if ringed is not None:
        args.append(ringed)
        specs.append(pl.BlockSpec(ringed.shape, lambda i: (0, 0)))
    if extra is not None:
        for e in extra:
            args.append(e)
            specs.append(pl.BlockSpec(e.shape, lambda i: (0, 0)))
    width = n + (128 if extra is not None else 0)
    return pl.pallas_call(
        functools.partial(part_kernel, ringed is not None, extra is not None),
        grid=(1,),
        in_specs=specs,
        out_specs=pl.BlockSpec((rows, width), lambda i: (0, 0)),
        out_shape=jax.ShapeDtypeStruct((rows, width), dtype),
        compiler_params=params(),
        cost_estimate=pl.CostEstimate(
            flops=2 * rows * 256 * n, bytes_accessed=2 * n * (k + 3 * rows), transcendentals=0
        ),
        name="part",
    )(*args)


def on_device(
    tokens,
    token_adapter,
    adapter_slot_table,
    gate_matrix,
    up_matrix,
    down_matrix,
    adapter_entry_maps,
    adapter_gate_exit,
    adapter_up_exit,
    adapter_down_entry,
    adapter_down_exit,
):
    units = gate_matrix.shape[1]
    a = lax.axis_index("adapter")
    t = lax.axis_index("tensor")
    y, z, x, c = a // 4, a % 4, t // 2, t % 2
    way = 1 - 2 * c

    every = lax.all_gather(tokens, AXES, axis=0, tiled=False).reshape(16, 8, 64, 1024)
    ids = lax.all_gather(token_adapter, "adapter", axis=0, tiled=True)

    names = jnp.arange(32, dtype=jnp.int32)
    member = ids[:, None] == names[None, :]
    order = jnp.arange(1024, dtype=jnp.int32)
    before = (order[:, None] > order[None, :]).astype(BF)
    earlier = jnp.dot(before, member.astype(BF), preferred_element_type=F32).astype(jnp.int32)
    rank_in = jnp.sum(jnp.where(member, earlier, 0), axis=1)
    slot = jnp.sum(jnp.where(member, adapter_slot_table[None, :], 0), axis=1)
    owner = slot // 2
    row = (slot % 2) * SEGMENT + rank_in
    select = (
        (jnp.where(owner == a, row, -1))[None, :] == jnp.arange(160, dtype=jnp.int32)[:, None]
    ).astype(BF).reshape(2, SEGMENT, 1024)
    relative = ((owner % 4 - z) % 4) * 4 + (owner // 4 - y) % 4
    pick = (
        (relative * 160 + row)[:, None] == jnp.arange(2560, dtype=jnp.int32)[None, :]
    ).astype(BF)
    mask = (slot[:, None] == (jnp.arange(2048, dtype=jnp.int32) // 64)[None, :]).astype(BF)

    def column(r, core):
        at = ((x + r) % 4 * 2 + core) * 1024
        return lax.dynamic_slice(down_matrix, (0, at), (units, 1024))

    chunks = ((1, 2), (3, 0))
    mine = [jnp.concatenate([column(r, c) for r in ch], axis=1) for ch in chunks]
    theirs = jnp.concatenate([column(r, 1 - c) for ch in chunks for r in ch], axis=1)
    entry_four = (
        adapter_down_entry.reshape(8, 4, units, 64).transpose(0, 2, 1, 3).reshape(8, units, 256)
    )

    low_own = low_own_rows(every, adapter_entry_maps, select).reshape(160, 128)
    low = jnp.stack([low_own] + [send(low_own, dy=-d) for d in (1, 2, 3)])
    low = jnp.stack([low] + [send(low, dz=-d) for d in (1, 2, 3)]).reshape(2560, 128)
    gate, up = gate_up(every, gate_matrix, up_matrix)

    exit_in, _ = lax.optimization_barrier((adapter_down_exit, low_own))
    exits = lax.all_gather(exit_in, "adapter", axis=0, tiled=True).reshape(2048, 1024)

    quarter = jnp.arange(4, dtype=jnp.int32)
    place = jnp.concatenate([way * (y - quarter) % 4, way * (z - quarter) % 4])
    hidden, extra = hidden_rows(
        place,
        gate,
        up,
        pick,
        mask,
        low,
        adapter_gate_exit.reshape(2048, units),
        adapter_up_exit.reshape(2048, units),
        entry_four,
    )
    back = np.array([0, 3, 2, 1])

    def block(v, color, r):
        v = v[:, r, :32] if color == 0 else v[r, :, 32:]
        return v.reshape(128, v.shape[-1])

    def back_block(v, color, r):
        r = int(back[r])
        v = v[:, r, :32] if color == 0 else v[r, :, 32:]
        v = jnp.stack([v[int(b)] for b in back])
        return v.reshape(128, v.shape[-1])

    turn = (1, 2, 3, 0)
    other = {}
    for r in turn:
        rows = jnp.concatenate([back_block(hidden, 0, r), back_block(hidden, 1, r)])
        product = jnp.dot(rows, theirs, preferred_element_type=F32).astype(BF)
        other[r] = send(product, dc=1)
    theirs_extra = send(
        jnp.stack([jnp.stack([back_block(extra, k, r) for r in range(4)]) for k in range(2)]).astype(BF),
        dc=1,
    )

    axes = (("z", "y"), ("y", "z"))
    state = {}
    for r in turn:
        for ch in range(2):
            for color in range(2):
                ringed = None if r == 1 else ring(state[ch, color], axes[color][0])
                own_extra = (
                    (block(extra, color, r), theirs_extra[color, r]) if ch == 1 else None
                )
                state[ch, color] = part(
                    block(hidden, color, r),
                    mine[ch],
                    other[r],
                    color,
                    ch,
                    ringed,
                    own_extra,
                    F32 if r == 0 else BF,
                )
    for ch in range(2):
        for color in range(2):
            held = state[ch, color].reshape(4, 32, -1)
            running = held[1]
            for r in (2, 3, 0):
                running = held[r] + ring(running.astype(BF), axes[color][1]).astype(F32)
            state[ch, color] = running
    summed = [jnp.concatenate([state[ch, 0], state[ch, 1]]) for ch in range(2)]
    tail = summed[1][:, 2048:]
    blocks = {
        1: summed[0][:, :1024],
        2: summed[0][:, 1024:],
        3: summed[1][:, :1024],
        0: summed[1][:, 1024:2048],
    }
    total = jnp.concatenate([blocks[0], tail], axis=1)
    for r in (1, 2, 3):
        total = total + send(
            jnp.concatenate([blocks[r], tail], axis=1).astype(BF), dx=r
        ).astype(F32)

    own_slot = jnp.sum(
        jnp.where(token_adapter[:, None] == names[None, :], adapter_slot_table[None, :], 0), axis=1
    )
    low_down = total[:, 1024:].astype(BF)
    spread = jnp.tile(low_down, (1, 16))
    spread = jnp.where(
        (own_slot // 2)[:, None] == (jnp.arange(2048, dtype=jnp.int32) // 128)[None, :], spread, 0
    )
    delta = jnp.dot(spread, exits, preferred_element_type=F32)
    return (total[:, :1024] + delta).astype(BF)


def solution(mesh):
    return jax.shard_map(
        on_device,
        mesh=mesh,
        in_specs=(
            P("adapter", "tensor"),
            P("adapter"),
            P(),
            P(None, ("adapter", "tensor")),
            P(None, ("adapter", "tensor")),
            P(("adapter", "tensor"), None),
            P("adapter", None, None),
            P(None, None, ("adapter", "tensor")),
            P(None, None, ("adapter", "tensor")),
            P(None, ("adapter", "tensor"), None),
            P("adapter", None, "tensor"),
        ),
        out_specs=P("adapter", "tensor"),
        check_vma=False,
    )
```

time: 564 us -> 302 us (0.54)
  waiting for transfers between devices: 332 us -> 78.8 us
  blocking collectives: 114 us -> 17.5 us
  Pallas kernels: 0 us -> 84.5 us
  starting transfers between devices: 0.16 us -> 36.2 us
  matrix products: 43 us -> 11.3 us
  local copies, waits for them, and re-layouts: 46.7 us -> 40.3 us
    reduce_scatter x2 -> x0, waiting for transfers between devices: 144 us -> none  [the longest x1 113 us: on_device(): lax.psum_scatter(product, 'adapter', scatter_dimension=0, tiled=True)]
    all_gather x3 -> x2, waiting for transfers between devices: 187 us -> 53.7 us  [the longest x1 52.8 us: on_device(): lax.all_gather(tokens, AXES, axis=0, tiled=False).reshape(16, 8, 64, 1024)]
    pallas_call x0 -> x19, Pallas kernels: none -> 84.5 us  [the longest x16 42.6 us: part(): pl.pallas_call(functools.partial(part_kernel, ringed is not None, extra i...]
    psum x1 -> x0, blocking collectives: 74 us -> none  [on_device(): down_total = lax.psum(down_part, ('adapter', 'tensor'))]
    gather x7 -> x0, local copies, waits for them, and re-layouts: 39 us -> none  [the longest x1 14 us: on_device(): every_rows[jnp.minimum(own_tokens, token_count - 1)]]
    ppermute x0 -> x38, starting transfers between devices: none -> 36.2 us  [the longest x24 21 us: ring(): return lax.ppermute(value, AXES, pairs(move))]
    dot_general x8 -> x6, matrix products: 43 us -> 11.3 us  [the longest x4 7.03 us: on_device(): product = jnp.dot(rows, theirs, preferred_element_type=F32).astype(BF)]
    ppermute x0 -> x38, waiting for transfers between devices: none -> 24.4 us  [the longest x24 16.9 us: ring(): return lax.ppermute(value, AXES, pairs(move))]
  transfers between devices with their start and end apart: 5 -> 40, of which waited for: 5 -> 15; matrix products, arithmetic and copies ran while one was open for 6% -> 16% of each run, Pallas kernels for 0% -> 20%
where the time goes in v1:
time: 302 us; the launch traced here: 299 us
  Pallas kernels  84.5 us (28%)
  waiting for transfers between devices  78.8 us (26%)
  local copies, waits for them, and re-layouts  40.3 us (13%)
  starting transfers between devices  36.2 us (12%)
  blocking collectives  17.5 us (6%)
  other arithmetic  15.8 us (5%)
  between operations  14.7 us (5%)
  matrix products  11.3 us (4%)
    all_gather x1, waiting for transfers between devices, on_device(): lax.all_gather(tokens, AXES, axis=0, tiled=False).reshape(16, 8, 64, 1024)  52.8 us
    pallas_call x16, Pallas kernels, part(): pl.pallas_call(functools.partial(part_kernel, ringed is not None, extra i...  42.6 us
    unnamed x55, local copies, waits for them, and re-layouts  24.7 us
    ppermute x24, starting transfers between devices, ring(): return lax.ppermute(value, AXES, pairs(move))  21 us
    unnamed x1, blocking collectives  17.5 us
    ppermute x24, waiting for transfers between devices, ring(): return lax.ppermute(value, AXES, pairs(move))  16.9 us
    pallas_call x1, Pallas kernels, gate_up(): pl.pallas_call(gate_up_kernel, grid=(8,), in_specs=[pl.BlockSpec((16, 1,...  16.1 us
    ppermute x14, starting transfers between devices, send(): lax.ppermute(value, AXES, pairs(lambda y, z, x, c: (y + dy, z + dz, x + d...  15.2 us
  transfers between devices with their start and end apart: 40, of which 15 were waited for; matrix products, arithmetic and copies ran while one was open for 16% of the time, Pallas kernels for 20%

profile of v1, /device:TPU:0, one launch (start us, length us, event | category | flops | bytes accessed | tf_op | source)
XLA Modules:
  0.0 299.2 jit_solution(7925852708525464769)
XLA Ops:
  10.3 17.5 %all-reduce = s32[1024]{0:T(1024)S(1)} all-reduce(s32[1024]{0:T(1024)S(1)} %dynamic-update-slice), channel_id=1, replica_groups=mesh['adapter'=16,'tensor'=8] {'adapter'}, use_global_device_ids=true, to_apply=%add | all-reduce | flops 1024 | bytes 8192
  29.1 2.5 constant_dynamic-slice_fusion.1
  34.5 2.8 compare_convert_fusion.m_ref
  37.2 3.3 %fusion.q_ref = bf16[1024,2560]{1,0:T(8,128)(2,1)} fusion(s32[1024]{0:T(1024)S(1)} %get-tuple-element.118), kind=kLoop, calls=%fused_computation.1 | loop fusion | flops 5242880 | bytes 5246976 | tf_op jit(solution)/shard_map/convert_element_type | solution.py:267
  40.5 52.8 %all-gather.6.cloned.1.call-done = bf16[8192,1024]{1,0:T(8,128)(2,1)} async-done(((bf16[64,1024]{1,0:T(8,128)(2,1)}), bf16[8192,1024]{1,0:T(8,128)(2,1)}) %all-gather.6.cloned.1.call-update) | async-done | bytes 16777232 | tf_op jit(solution)/shard_map/all_gather | solution.py:249
  93.3 14.9 %low_own.1 = bf16[2,80,128]{2,1,0:T(8,128)(2,1)} custom-call(bf16[16,8,64,1024]{3,2,1,0:T(8,128)(2,1)} %bitcast.208, bf16[2,8192,128]{2,1,0:T(8,128)(2,1)} %e_ref.1, bf16[2,80,1024]{2,1,0:T(8,128)(2,1)} %compare_convert_fusion.1.s_ref), custom_call_target="tpu_custom_call" | custom-call | flops 4294967296 | bytes 22020096 | tf_op jit(solution)/shard_map/low_own/pallas_call | solution.py:65
  109.7 2.7 collective-permute-start.1
  114.5 6.2 %copy.21.g_ref = bf16[8192,224]{1,0:T(8,128)(2,1)} copy(bf16[8192,224]{0,1:T(8,128)(2,1)} %param.14) | data formatting | bytes 7340032 | tf_op args[3]
  120.7 6.3 %copy.22.u_ref = bf16[8192,224]{1,0:T(8,128)(2,1)} copy(bf16[8192,224]{0,1:T(8,128)(2,1)} %param.15) | data formatting | bytes 7340032 | tf_op args[4]
  129.6 2.9 collective-permute-start.4
  133.8 16.1 %gate_up.1 = (f32[1024,224]{1,0:T(8,128)}, f32[1024,224]{1,0:T(8,128)}) custom-call(bf16[16,8,64,1024]{3,2,1,0:T(8,128)(2,1)} %bitcast.209, bf16[8192,224]{1,0:T(8,128)(2,1)} %copy.21.g_ref, bf16[8192,224]{1,0:T(8,128)(2,1)} %copy.22.u_ref), custom_call_target="tpu_custom_call" | custom-call | flops 8589934592 | bytes 26214400 | tf_op jit(solution)/shard_map/gate_up/pallas_call | solution.py:99
  150.8 11.0 %hidden_rows.1 = (bf16[4,4,64,224]{3,2,1,0:T(8,128)(2,1)}, f32[4,4,64,128]{3,2,1,0:T(8,128)}) custom-call(s32[8]{0:T(128)} %pad_add_fusion.place, f32[1024,224]{1,0:T(8,128)} %get-tuple-element.10.g_ref, f32[1024,224]{1,0:T(8,128)} %get-tuple-element.11.u_ref, bf16[1024,2560]{1,0:T(8,128)(2,1)} %fusion.q_ref, bf16[1024,2048]{1,0:T(8,128)(2,1)} %compare_convert_fusion.m_ref, ...), custom_call_target="tpu_custom_call" | custom-call | flops 2684354560 | bytes 16777216 | tf_op jit(solution)/shard_map/hidden_rows/pallas_call | solution.py:145
  182.3 2.5 part.16
  186.1 2.5 part.20
  188.6 2.5 part.24
  191.9 2.6 part.29
  196.5 2.7 part.17
  200.4 2.7 part.21
  204.8 2.7 part.25
  210.6 2.7 part.30
  214.9 2.7 part.18
  219.3 2.7 part.22
  223.6 2.6 part.26
  228.1 2.8 part.31
  233.4 3.4 %collective-permute-done.25.refs_3_ = bf16[128,2048]{1,0:T(8,128)(2,1)S(1)} collective-permute-done((bf16[128,2048]{1,0:T(8,128)(2,1)}, bf16[128,2048]{1,0:T(8,128)(2,1)S(1)}, u32[]{:S(2)}, u32[]{:S(2)}) %collective-permute-start.25) | collective-permute-done | bytes 524320 | tf_op jit(solution)/shard_map/ppermute | solution.py:36
  237.6 2.8 part.27
  244.1 2.9 part.19
  250.8 2.9 part.23
  268.5 4.1 %collective-permute-done.34 = bf16[32,2048]{1,0:T(8,128)(2,1)S(1)} collective-permute-done((bf16[32,2048]{1,0:T(8,128)(2,1)S(1)}, bf16[32,2048]{1,0:T(8,128)(2,1)S(1)}, u32[]{:S(2)}, u32[]{:S(2)}) %collective-permute-start.34) | collective-permute-done | bytes 131104 | tf_op jit(solution)/shard_map/ppermute | solution.py:36
  273.4 4.4 %collective-permute-done.16 = bf16[32,2176]{1,0:T(8,128)(2,1)S(1)} collective-permute-done((bf16[32,2176]{1,0:T(8,128)(2,1)S(1)}, bf16[32,2176]{1,0:T(8,128)(2,1)S(1)}, u32[]{:S(2)}, u32[]{:S(2)}) %collective-permute-start.16) | collective-permute-done | bytes 139296 | tf_op jit(solution)/shard_map/ppermute | solution.py:36
  283.1 3.0 collective-permute-done.36
  288.7 3.7 %fusion.16 = bf16[64,1024]{1,0:T(8,128)(2,1)} fusion(f32[64,1152]{1,0:T(8,128)S(1)} %fusion.8, bf16[2048,1024]{1,0:T(8,128)(2,1)} %bitcast.210, bf16[8,8,16,128]{3,2,1,0:T(8,128)(2,1)S(1)} %bitcast.214), kind=kOutput, calls=%fused_computation.43 | convolution fusion | flops 268566528 | bytes 4849664 | tf_op jit(solution)/shard_map/dot_general | solution.py:373
  (202 shorter events, 86.9 us)
Async XLA Ops:
  6.5 86.8 %all-gather.6.cloned.1.call-start = ((), (), s32[]{:S(2)}) async-start(), calls=%async_computation.1 | async-start | bytes 16908288 | tf_op jit(solution)/shard_map/all_gather | solution.py:249
  7.3 281.4 %all-gather.4.cloned.1.call-start = ((), (), s32[]{:S(2)}) async-start(), calls=%async_computation | async-start | bytes 4456448 | tf_op jit(solution)/shard_map/all_gather | solution.py:287
  108.2 20.2 %collective-permute-start.2 = (bf16[160,128]{1,0:T(8,128)(2,1)}, bf16[160,128]{1,0:T(8,128)(2,1)S(1)}, u32[]{:S(2)}, u32[]{:S(2)}) collective-permute-start(bf16[160,128]{1,0:T(8,128)(2,1)} %bitcast.240), channel_id=1, source_target_pairs={{0,32},{1,33},{2,34},{3,35},{4,36},{5,37},{6,38},{7,39},{8,40},{9,... | collective-permute-start | bytes 122888 | tf_op jit(solution)/shard_map/ppermute | solution.py:28
  109.7 18.7 %collective-permute-start.1 = (bf16[160,128]{1,0:T(8,128)(2,1)}, bf16[160,128]{1,0:T(8,128)(2,1)S(1)}, u32[]{:S(2)}, u32[]{:S(2)}) collective-permute-start(bf16[160,128]{1,0:T(8,128)(2,1)} %bitcast.241), channel_id=1, source_target_pairs={{0,64},{1,65},{2,66},{3,67},{4,68},{5,69},{6,70},{7,71},{8,72},{9,... | collective-permute-start | bytes 122888 | tf_op jit(solution)/shard_map/ppermute | solution.py:28
  112.4 15.9 %collective-permute-start = (bf16[160,128]{1,0:T(8,128)(2,1)}, bf16[160,128]{1,0:T(8,128)(2,1)S(1)}, u32[]{:S(2)}, u32[]{:S(2)}) collective-permute-start(bf16[160,128]{1,0:T(8,128)(2,1)} %bitcast.242), channel_id=1, source_target_pairs={{0,96},{1,97},{2,98},{3,99},{4,100},{5,101},{6,102},{7,103},{8,104... | collective-permute-start | bytes 122888 | tf_op jit(solution)/shard_map/ppermute | solution.py:28
  128.4 21.4 %collective-permute-start.5 = (bf16[4,160,128]{2,1,0:T(8,128)(2,1)S(1)}, bf16[4,160,128]{2,1,0:T(8,128)(2,1)S(1)}, u32[]{:S(2)}, u32[]{:S(2)}) collective-permute-start(bf16[4,160,128]{2,1,0:T(8,128)(2,1)S(1)} %get-tuple-element.114), channel_id=1, source_target_pairs={{0,8},{1,9},{2,10},{3,11},{4,12},{5,13},{6,14},{7,15},{8,16},{9,17... | collective-permute-start | bytes 491528 | tf_op jit(solution)/shard_map/ppermute | solution.py:28
  129.6 20.3 %collective-permute-start.4 = (bf16[4,160,128]{2,1,0:T(8,128)(2,1)S(1)}, bf16[4,160,128]{2,1,0:T(8,128)(2,1)S(1)}, u32[]{:S(2)}, u32[]{:S(2)}) collective-permute-start(bf16[4,160,128]{2,1,0:T(8,128)(2,1)S(1)} %get-tuple-element.114), channel_id=1, source_target_pairs={{0,16},{1,17},{2,18},{3,19},{4,20},{5,21},{6,22},{7,23},{8,24},{9,... | collective-permute-start | bytes 491528 | tf_op jit(solution)/shard_map/ppermute | solution.py:28
  132.4 17.4 %collective-permute-start.3 = (bf16[4,160,128]{2,1,0:T(8,128)(2,1)S(1)}, bf16[4,160,128]{2,1,0:T(8,128)(2,1)S(1)}, u32[]{:S(2)}, u32[]{:S(2)}) collective-permute-start(bf16[4,160,128]{2,1,0:T(8,128)(2,1)S(1)} %get-tuple-element.114), channel_id=1, source_target_pairs={{0,24},{1,25},{2,26},{3,27},{4,28},{5,29},{6,30},{7,31},{8,0},{9,1... | collective-permute-start | bytes 491528 | tf_op jit(solution)/shard_map/ppermute | solution.py:28
  165.8 41.6 %collective-permute-start.7 = (bf16[256,4096]{1,0:T(8,128)(2,1)}, bf16[256,4096]{1,0:T(8,128)(2,1)}, u32[]{:S(2)}, u32[]{:S(2)}) collective-permute-start(bf16[256,4096]{1,0:T(8,128)(2,1)} %convolution_convert_fusion.2), channel_id=1, source_target_pairs={{0,1},{1,0},{2,3},{3,2},{4,5},{5,4},{6,7},{7,6},{8,9},{9,8},{10,11... | collective-permute-start | bytes 6291464 | tf_op jit(solution)/shard_map/ppermute | solution.py:28
  168.0 20.6 %collective-permute-start.8 = (bf16[256,4096]{1,0:T(8,128)(2,1)}, bf16[256,4096]{1,0:T(8,128)(2,1)}, u32[]{:S(2)}, u32[]{:S(2)}) collective-permute-start(bf16[256,4096]{1,0:T(8,128)(2,1)} %convolution_convert_fusion.1), channel_id=1, source_target_pairs={{0,1},{1,0},{2,3},{3,2},{4,5},{5,4},{6,7},{7,6},{8,9},{9,8},{10,11... | collective-permute-start | bytes 6291464 | tf_op jit(solution)/shard_map/ppermute | solution.py:28
  170.6 10.0 %collective-permute-start.10 = (bf16[2,4,128,128]{3,2,1,0:T(8,128)(2,1)}, bf16[2,4,128,128]{3,2,1,0:T(8,128)(2,1)}, u32[]{:S(2)}, u32[]{:S(2)}) collective-permute-start(bf16[2,4,128,128]{3,2,1,0:T(8,128)(2,1)} %pad_maximum_fusion.5), channel_id=1, source_target_pairs={{0,1},{1,0},{2,3},{3,2},{4,5},{5,4},{6,7},{7,6},{8,9},{9,8},{10,11... | collective-permute-start | bytes 786440 | tf_op jit(solution)/shard_map/ppermute | solution.py:28
  174.5 52.8 %collective-permute-start.6 = (bf16[256,4096]{1,0:T(8,128)(2,1)}, bf16[256,4096]{1,0:T(8,128)(2,1)}, u32[]{:S(2)}, u32[]{:S(2)}) collective-permute-start(bf16[256,4096]{1,0:T(8,128)(2,1)} %convolution_convert_fusion.3), channel_id=1, source_target_pairs={{0,1},{1,0},{2,3},{3,2},{4,5},{5,4},{6,7},{7,6},{8,9},{9,8},{10,11... | collective-permute-start | bytes 6291464 | tf_op jit(solution)/shard_map/ppermute | solution.py:28
  180.1 11.0 %collective-permute-start.29 = (bf16[128,2048]{1,0:T(8,128)(2,1)}, bf16[128,2048]{1,0:T(8,128)(2,1)S(1)}, u32[]{:S(2)}, u32[]{:S(2)}) collective-permute-start(bf16[128,2048]{1,0:T(8,128)(2,1)} %part.28), channel_id=1, source_target_pairs={{0,32},{1,97},{2,34},{3,99},{4,36},{5,101},{6,38},{7,103},{8,40},{... | collective-permute-start | bytes 1572872 | tf_op jit(solution)/shard_map/ppermute | solution.py:36
  184.8 11.0 %collective-permute-start.11 = (bf16[128,2176]{1,0:T(8,128)(2,1)}, bf16[128,2176]{1,0:T(8,128)(2,1)S(1)}, u32[]{:S(2)}, u32[]{:S(2)}) collective-permute-start(bf16[128,2176]{1,0:T(8,128)(2,1)} %part.16), channel_id=1, source_target_pairs={{0,8},{1,25},{2,10},{3,27},{4,12},{5,29},{6,14},{7,31},{8,16},{9,1... | collective-permute-start | bytes 1671176 | tf_op jit(solution)/shard_map/ppermute | solution.py:36
  188.6 11.0 %collective-permute-start.17 = (bf16[128,2176]{1,0:T(8,128)(2,1)}, bf16[128,2176]{1,0:T(8,128)(2,1)S(1)}, u32[]{:S(2)}, u32[]{:S(2)}) collective-permute-start(bf16[128,2176]{1,0:T(8,128)(2,1)} %part.20), channel_id=1, source_target_pairs={{0,32},{1,97},{2,34},{3,99},{4,36},{5,101},{6,38},{7,103},{8,40},{... | collective-permute-start | bytes 1671176 | tf_op jit(solution)/shard_map/ppermute | solution.py:36
  191.1 12.0 %collective-permute-start.23 = (bf16[128,2048]{1,0:T(8,128)(2,1)}, bf16[128,2048]{1,0:T(8,128)(2,1)S(1)}, u32[]{:S(2)}, u32[]{:S(2)}) collective-permute-start(bf16[128,2048]{1,0:T(8,128)(2,1)} %part.24), channel_id=1, source_target_pairs={{0,8},{1,25},{2,10},{3,27},{4,12},{5,29},{6,14},{7,31},{8,16},{9,1... | collective-permute-start | bytes 1572872 | tf_op jit(solution)/shard_map/ppermute | solution.py:36
  195.7 14.1 %collective-permute-start.30 = (bf16[128,2048]{1,0:T(8,128)(2,1)}, bf16[128,2048]{1,0:T(8,128)(2,1)S(1)}, u32[]{:S(2)}, u32[]{:S(2)}) collective-permute-start(bf16[128,2048]{1,0:T(8,128)(2,1)} %part.29), channel_id=1, source_target_pairs={{0,32},{1,97},{2,34},{3,99},{4,36},{5,101},{6,38},{7,103},{8,40},{... | collective-permute-start | bytes 1572872 | tf_op jit(solution)/shard_map/ppermute | solution.py:36
  199.6 14.5 %collective-permute-start.12 = (bf16[128,2176]{1,0:T(8,128)(2,1)}, bf16[128,2176]{1,0:T(8,128)(2,1)S(1)}, u32[]{:S(2)}, u32[]{:S(2)}) collective-permute-start(bf16[128,2176]{1,0:T(8,128)(2,1)} %part.17), channel_id=1, source_target_pairs={{0,8},{1,25},{2,10},{3,27},{4,12},{5,29},{6,14},{7,31},{8,16},{9,1... | collective-permute-start | bytes 1671176 | tf_op jit(solution)/shard_map/ppermute | solution.py:36
  203.1 15.4 %collective-permute-start.18 = (bf16[128,2176]{1,0:T(8,128)(2,1)}, bf16[128,2176]{1,0:T(8,128)(2,1)S(1)}, u32[]{:S(2)}, u32[]{:S(2)}) collective-permute-start(bf16[128,2176]{1,0:T(8,128)(2,1)} %part.21), channel_id=1, source_target_pairs={{0,32},{1,97},{2,34},{3,99},{4,36},{5,101},{6,38},{7,103},{8,40},{... | collective-permute-start | bytes 1671176 | tf_op jit(solution)/shard_map/ppermute | solution.py:36
  207.4 15.3 %collective-permute-start.24 = (bf16[128,2048]{1,0:T(8,128)(2,1)}, bf16[128,2048]{1,0:T(8,128)(2,1)S(1)}, u32[]{:S(2)}, u32[]{:S(2)}) collective-permute-start(bf16[128,2048]{1,0:T(8,128)(2,1)} %part.25), channel_id=1, source_target_pairs={{0,8},{1,25},{2,10},{3,27},{4,12},{5,29},{6,14},{7,31},{8,16},{9,1... | collective-permute-start | bytes 1572872 | tf_op jit(solution)/shard_map/ppermute | solution.py:36
  213.3 13.9 %collective-permute-start.31 = (bf16[128,2048]{1,0:T(8,128)(2,1)}, bf16[128,2048]{1,0:T(8,128)(2,1)S(1)}, u32[]{:S(2)}, u32[]{:S(2)}) collective-permute-start(bf16[128,2048]{1,0:T(8,128)(2,1)} %part.30), channel_id=1, source_target_pairs={{0,32},{1,97},{2,34},{3,99},{4,36},{5,101},{6,38},{7,103},{8,40},{... | collective-permute-start | bytes 1572872 | tf_op jit(solution)/shard_map/ppermute | solution.py:36
  217.6 25.7 %collective-permute-start.13 = (bf16[128,2176]{1,0:T(8,128)(2,1)}, bf16[128,2176]{1,0:T(8,128)(2,1)S(1)}, u32[]{:S(2)}, u32[]{:S(2)}) collective-permute-start(bf16[128,2176]{1,0:T(8,128)(2,1)} %part.18), channel_id=1, source_target_pairs={{0,8},{1,25},{2,10},{3,27},{4,12},{5,29},{6,14},{7,31},{8,16},{9,1... | collective-permute-start | bytes 1671176 | tf_op jit(solution)/shard_map/ppermute | solution.py:36
  222.0 28.0 %collective-permute-start.19 = (bf16[128,2176]{1,0:T(8,128)(2,1)}, bf16[128,2176]{1,0:T(8,128)(2,1)S(1)}, u32[]{:S(2)}, u32[]{:S(2)}) collective-permute-start(bf16[128,2176]{1,0:T(8,128)(2,1)} %part.22), channel_id=1, source_target_pairs={{0,32},{1,97},{2,34},{3,99},{4,36},{5,101},{6,38},{7,103},{8,40},{... | collective-permute-start | bytes 1671176 | tf_op jit(solution)/shard_map/ppermute | solution.py:36
  226.2 10.6 %collective-permute-start.25 = (bf16[128,2048]{1,0:T(8,128)(2,1)}, bf16[128,2048]{1,0:T(8,128)(2,1)S(1)}, u32[]{:S(2)}, u32[]{:S(2)}) collective-permute-start(bf16[128,2048]{1,0:T(8,128)(2,1)} %part.26), channel_id=1, source_target_pairs={{0,8},{1,25},{2,10},{3,27},{4,12},{5,29},{6,14},{7,31},{8,16},{9,1... | collective-permute-start | bytes 1572872 | tf_op jit(solution)/shard_map/ppermute | solution.py:36
  232.5 22.3 %collective-permute-start.32 = (bf16[32,2048]{1,0:T(8,128)(2,1)}, bf16[32,2048]{1,0:T(8,128)(2,1)}, u32[]{:S(2)}, u32[]{:S(2)}) collective-permute-start(bf16[32,2048]{1,0:T(8,128)(2,1)} %slice.1024), channel_id=1, source_target_pairs={{0,8},{1,25},{2,10},{3,27},{4,12},{5,29},{6,14},{7,31},{8,16},{9,1... | collective-permute-start | bytes 393224 | tf_op jit(solution)/shard_map/ppermute | solution.py:36
  242.0 14.1 %collective-permute-start.26 = (bf16[32,2048]{1,0:T(8,128)(2,1)}, bf16[32,2048]{1,0:T(8,128)(2,1)}, u32[]{:S(2)}, u32[]{:S(2)}) collective-permute-start(bf16[32,2048]{1,0:T(8,128)(2,1)} %slice.1025), channel_id=1, source_target_pairs={{0,32},{1,97},{2,34},{3,99},{4,36},{5,101},{6,38},{7,103},{8,40},{... | collective-permute-start | bytes 393224 | tf_op jit(solution)/shard_map/ppermute | solution.py:36
  248.1 10.2 %collective-permute-start.14 = (bf16[32,2176]{1,0:T(8,128)(2,1)S(1)}, bf16[32,2176]{1,0:T(8,128)(2,1)S(1)}, u32[]{:S(2)}, u32[]{:S(2)}) collective-permute-start(bf16[32,2176]{1,0:T(8,128)(2,1)S(1)} %slice.1023), channel_id=1, source_target_pairs={{0,32},{1,97},{2,34},{3,99},{4,36},{5,101},{6,38},{7,103},{8,40},{... | collective-permute-start | bytes 417800 | tf_op jit(solution)/shard_map/ppermute | solution.py:36
  257.1 7.4 %collective-permute-start.27 = (bf16[32,2048]{1,0:T(8,128)(2,1)S(1)}, bf16[32,2048]{1,0:T(8,128)(2,1)S(1)}, u32[]{:S(2)}, u32[]{:S(2)}) collective-permute-start(bf16[32,2048]{1,0:T(8,128)(2,1)S(1)} %fusion.20), channel_id=1, source_target_pairs={{0,32},{1,97},{2,34},{3,99},{4,36},{5,101},{6,38},{7,103},{8,40},{... | collective-permute-start | bytes 393224 | tf_op jit(solution)/shard_map/ppermute | solution.py:36
  262.5 10.1 %collective-permute-start.34 = (bf16[32,2048]{1,0:T(8,128)(2,1)S(1)}, bf16[32,2048]{1,0:T(8,128)(2,1)S(1)}, u32[]{:S(2)}, u32[]{:S(2)}) collective-permute-start(bf16[32,2048]{1,0:T(8,128)(2,1)S(1)} %fusion.19), channel_id=1, source_target_pairs={{0,8},{1,25},{2,10},{3,27},{4,12},{5,29},{6,14},{7,31},{8,16},{9,1... | collective-permute-start | bytes 393224 | tf_op jit(solution)/shard_map/ppermute | solution.py:36
  264.5 8.8 %collective-permute-start.28 = (bf16[32,2048]{1,0:T(8,128)(2,1)S(1)}, bf16[32,2048]{1,0:T(8,128)(2,1)S(1)}, u32[]{:S(2)}, u32[]{:S(2)}) collective-permute-start(bf16[32,2048]{1,0:T(8,128)(2,1)S(1)} %fusion.21), channel_id=1, source_target_pairs={{0,32},{1,97},{2,34},{3,99},{4,36},{5,101},{6,38},{7,103},{8,40},{... | collective-permute-start | bytes 393224 | tf_op jit(solution)/shard_map/ppermute | solution.py:36
  265.8 12.0 %collective-permute-start.16 = (bf16[32,2176]{1,0:T(8,128)(2,1)S(1)}, bf16[32,2176]{1,0:T(8,128)(2,1)S(1)}, u32[]{:S(2)}, u32[]{:S(2)}) collective-permute-start(bf16[32,2176]{1,0:T(8,128)(2,1)S(1)} %fusion.12), channel_id=1, source_target_pairs={{0,32},{1,97},{2,34},{3,99},{4,36},{5,101},{6,38},{7,103},{8,40},{... | collective-permute-start | bytes 417800 | tf_op jit(solution)/shard_map/ppermute | solution.py:36
  268.5 9.4 %collective-permute-start.22 = (bf16[32,2176]{1,0:T(8,128)(2,1)S(1)}, bf16[32,2176]{1,0:T(8,128)(2,1)S(1)}, u32[]{:S(2)}, u32[]{:S(2)}) collective-permute-start(bf16[32,2176]{1,0:T(8,128)(2,1)S(1)} %fusion.10), channel_id=1, source_target_pairs={{0,8},{1,25},{2,10},{3,27},{4,12},{5,29},{6,14},{7,31},{8,16},{9,1... | collective-permute-start | bytes 417800 | tf_op jit(solution)/shard_map/ppermute | solution.py:36
  (33 other events, 288.4 us)
Sparse Core Ops, SparseCore 0:
  10.5 82.7 all-gather.5
  233.6 55.0 all-gather.3

commit v2 on v1

v2 whole, which is shorter than its diff:
```python
import functools

import jax
import jax.numpy as jnp
from jax import lax
from jax.experimental import pallas as pl
from jax.experimental.pallas import tpu as pltpu
from jax.sharding import PartitionSpec as P

SEGMENT = 80
BF = jnp.bfloat16
F32 = jnp.float32
AXES = ("adapter", "tensor")
VMEM_LIMIT = 60 * 1024 * 1024


def pairs(move):
    out = []
    for i in range(128):
        y, z, x, c = i // 32, (i // 8) % 4, (i // 2) % 4, i % 2
        ty, tz, tx, tc = move(y, z, x, c)
        out.append((i, (ty % 4) * 32 + (tz % 4) * 8 + (tx % 4) * 2 + tc % 2))
    return out


def send(value, dy=0, dz=0, dx=0, dc=0):
    return lax.ppermute(value, AXES, pairs(lambda y, z, x, c: (y + dy, z + dz, x + dx, c + dc)))


def ring(value, axis):
    def move(y, z, x, c):
        d = 1 - 2 * c
        return (y + d, z, x, c) if axis == "y" else (y, z + d, x, c)

    return lax.ppermute(value, AXES, pairs(move))


def params(n=1):
    return pltpu.CompilerParams(
        dimension_semantics=("arbitrary",) * n, vmem_limit_bytes=VMEM_LIMIT
    )


def nt(a, b):
    return lax.dot_general(a, b, (((1,), (1,)), ((), ())), preferred_element_type=F32)


def low_kernel(x_ref, e_ref, s_ref, o_ref, acc):
    k = pl.program_id(0)

    @pl.when(k == 0)
    def _():
        acc[...] = jnp.zeros_like(acc)

    for j in range(2):
        x = x_ref[:, j].reshape(1024, 1024)
        at = pl.ds(1024 * j, 1024)
        e = jnp.concatenate([e_ref[0, at], e_ref[1, at]], axis=1)
        acc[...] += jnp.dot(x, e, preferred_element_type=F32)

    @pl.when(k == pl.num_programs(0) - 1)
    def _():
        for j in range(2):
            o_ref[j] = jnp.dot(
                s_ref[j], acc[:, 128 * j : 128 * (j + 1)].astype(BF), preferred_element_type=F32
            ).astype(BF)


def low_own_rows(every, entry, select):
    return pl.pallas_call(
        low_kernel,
        grid=(4,),
        in_specs=[
            pl.BlockSpec((16, 2, 64, 1024), lambda k: (0, k, 0, 0)),
            pl.BlockSpec((2, 2048, 128), lambda k: (0, k, 0)),
            pl.BlockSpec((2, SEGMENT, 1024), lambda k: (0, 0, 0)),
        ],
        out_specs=pl.BlockSpec((2, SEGMENT, 128), lambda k: (0, 0, 0)),
        out_shape=jax.ShapeDtypeStruct((2, SEGMENT, 128), BF),
        scratch_shapes=[pltpu.VMEM((1024, 256), F32)],
        compiler_params=params(),
        cost_estimate=pl.CostEstimate(
            flops=2 * 1024 * 8192 * 256, bytes_accessed=21 << 20, transcendentals=0
        ),
        name="low_own",
    )(every, entry, select)


def gate_up_kernel(x_ref, g_ref, u_ref, go_ref, uo_ref):
    k = pl.program_id(0)

    @pl.when(k == 0)
    def _():
        go_ref[...] = jnp.zeros_like(go_ref)
        uo_ref[...] = jnp.zeros_like(uo_ref)

    for j in range(2):
        x = x_ref[:, j].reshape(1024, 1024)
        at = pl.ds(1024 * j, 1024)
        go_ref[...] += nt(x, g_ref[:, at])
        uo_ref[...] += nt(x, u_ref[:, at])


def gate_up(every, gate, up):
    n = gate.shape[0]
    return pl.pallas_call(
        gate_up_kernel,
        grid=(4,),
        in_specs=[
            pl.BlockSpec((16, 2, 64, 1024), lambda k: (0, k, 0, 0)),
            pl.BlockSpec((n, 2048), lambda k: (0, k)),
            pl.BlockSpec((n, 2048), lambda k: (0, k)),
        ],
        out_specs=[pl.BlockSpec((1024, n), lambda k: (0, 0))] * 2,
        out_shape=[jax.ShapeDtypeStruct((1024, n), F32)] * 2,
        compiler_params=params(),
        cost_estimate=pl.CostEstimate(
            flops=2 * 1024 * 8192 * 512, bytes_accessed=25 << 20, transcendentals=0
        ),
        name="gate_up",
    )(every, gate, up)


def hidden_kernel(
    place, g_ref, u_ref, q_ref, m_ref, low_ref, ge_ref, ue_ref, de_ref, ha_ref, hb_ref, da_ref, db_ref
):
    low = jnp.dot(q_ref[...], low_ref[...], preferred_element_type=F32)
    lg = low[:, :64].astype(BF)
    lu = low[:, 64:].astype(BF)
    lg = jnp.concatenate([lg] * 4, axis=1)
    lu = jnp.concatenate([lu] * 4, axis=1)
    gate = g_ref[...]
    up = u_ref[...]
    for j in range(8):
        mask = m_ref[:, 256 * j : 256 * (j + 1)]
        gate += jnp.dot(lg * mask, ge_ref[pl.ds(256 * j, 256)], preferred_element_type=F32)
        up += jnp.dot(lu * mask, ue_ref[pl.ds(256 * j, 256)], preferred_element_type=F32)
    hidden = (gate / (1.0 + jnp.exp(-gate)) * up).astype(BF)
    down = jnp.zeros((256, 256), F32)
    for j in range(8):
        mask = m_ref[:, 256 * j : 256 * (j + 1)].astype(F32)
        down += nt(hidden, de_ref[pl.ds(256 * j, 256)]) * mask
    down = down[:, :128] + down[:, 128:]
    for z in range(4):
        at = place[4 + z]
        ha_ref[at, 0] = hidden[64 * z : 64 * z + 32]
        hb_ref[0, at] = hidden[64 * z + 32 : 64 * z + 64]
        da_ref[at, 0] = down[64 * z : 64 * z + 32]
        db_ref[0, at] = down[64 * z + 32 : 64 * z + 64]


def hidden_rows(place, gate, up, pick, mask, low, gate_exit, up_exit, down_entry):
    n = gate.shape[1]
    return pl.pallas_call(
        hidden_kernel,
        grid_spec=pltpu.PrefetchScalarGridSpec(
            num_scalar_prefetch=1,
            grid=(4,),
            in_specs=[
                pl.BlockSpec((256, n), lambda i, p: (i, 0)),
                pl.BlockSpec((256, n), lambda i, p: (i, 0)),
                pl.BlockSpec((256, 2560), lambda i, p: (i, 0)),
                pl.BlockSpec((256, 2048), lambda i, p: (i, 0)),
                pl.BlockSpec((2560, 128), lambda i, p: (0, 0)),
                pl.BlockSpec((2048, n), lambda i, p: (0, 0)),
                pl.BlockSpec((2048, n), lambda i, p: (0, 0)),
                pl.BlockSpec((2048, n), lambda i, p: (0, 0)),
            ],
            out_specs=[
                pl.BlockSpec((4, 1, 32, n), lambda i, p: (0, p[i], 0, 0)),
                pl.BlockSpec((1, 4, 32, n), lambda i, p: (p[i], 0, 0, 0)),
                pl.BlockSpec((4, 1, 32, 128), lambda i, p: (0, p[i], 0, 0)),
                pl.BlockSpec((1, 4, 32, 128), lambda i, p: (p[i], 0, 0, 0)),
            ],
        ),
        out_shape=[jax.ShapeDtypeStruct((4, 4, 32, n), BF)] * 2
        + [jax.ShapeDtypeStruct((4, 4, 32, 128), F32)] * 2,
        compiler_params=params(),
        cost_estimate=pl.CostEstimate(
            flops=2 * 1024 * 2560 * 512, bytes_accessed=16 << 20, transcendentals=1024 * n
        ),
        name="hidden_rows",
    )(place, gate, up, pick, mask, low, gate_exit, up_exit, down_entry)


WIDE = 4096 + 128
TILE = WIDE // 3


def turned(v):
    return jnp.concatenate([v[0, g] for g in (0, 3, 2, 1)], axis=0)


def straight(v):
    return v[0].reshape(128, v.shape[-1])


def part_kernel(arrange, with_other, ha_ref, hb_ref, da_ref, db_ref, w_ref, *refs):
    o_ref = refs[-1]
    rows = jnp.concatenate([arrange(ha_ref[...]), arrange(hb_ref[...])], axis=0)
    total = jnp.dot(rows, w_ref[...], preferred_element_type=F32).reshape(2, 128, TILE)
    if with_other:
        total += refs[0][0].astype(F32)
    o_ref[0] = total.astype(o_ref.dtype)

    @pl.when(pl.program_id(0) == 2)
    def _():
        extra = jnp.concatenate([arrange(da_ref[...]), arrange(db_ref[...])], axis=0)
        extra = extra.reshape(2, 128, 128)
        o_ref[0, :, :, TILE - 128 :] = (total[:, :, TILE - 128 :] + extra).astype(o_ref.dtype)


def part(ha, hb, da, db, w, other, first, count, back, dtype):
    n = ha.shape[-1]

    def at(t, i):
        r = (first + i) % 4
        return ((4 - r) % 4 if back else r), 0, 0, 0

    args = [ha, hb, da, db, w]
    specs = [
        pl.BlockSpec((1, 4, 32, n), at),
        pl.BlockSpec((1, 4, 32, n), at),
        pl.BlockSpec((1, 4, 32, 128), at),
        pl.BlockSpec((1, 4, 32, 128), at),
        pl.BlockSpec((n, TILE), lambda t, i: (0, t)),
    ]
    if other is not None:
        args.append(other)
        specs.append(pl.BlockSpec((1, 2, 128, TILE), lambda t, i: (i, 0, 0, t)))
    return pl.pallas_call(
        functools.partial(part_kernel, turned if back else straight, other is not None),
        grid=(3, count),
        in_specs=specs,
        out_specs=pl.BlockSpec((1, 2, 128, TILE), lambda t, i: (i, 0, 0, t)),
        out_shape=jax.ShapeDtypeStruct((count, 2, 128, WIDE), dtype),
        compiler_params=params(2),
        cost_estimate=pl.CostEstimate(
            flops=2 * 256 * 256 * WIDE * count,
            bytes_accessed=WIDE * 2 * (224 + 256 * count * 3),
            transcendentals=0,
        ),
        name="part",
    )(*args)


def on_device(
    tokens,
    token_adapter,
    adapter_slot_table,
    gate_matrix,
    up_matrix,
    down_matrix,
    adapter_entry_maps,
    adapter_gate_exit,
    adapter_up_exit,
    adapter_down_entry,
    adapter_down_exit,
):
    units = gate_matrix.shape[1]
    a = lax.axis_index("adapter")
    t = lax.axis_index("tensor")
    y, z, x, c = a // 4, a % 4, t // 2, t % 2
    way = 1 - 2 * c

    every = lax.all_gather(tokens, AXES, axis=0, tiled=False).reshape(16, 8, 64, 1024)
    ids = lax.all_gather(token_adapter, "adapter", axis=0, tiled=True)

    names = jnp.arange(32, dtype=jnp.int32)
    member = ids[:, None] == names[None, :]
    order = jnp.arange(1024, dtype=jnp.int32)
    before = (order[:, None] > order[None, :]).astype(BF)
    earlier = jnp.dot(before, member.astype(BF), preferred_element_type=F32).astype(jnp.int32)
    rank_in = jnp.sum(jnp.where(member, earlier, 0), axis=1)
    slot = jnp.sum(jnp.where(member, adapter_slot_table[None, :], 0), axis=1)
    owner = slot // 2
    row = (slot % 2) * SEGMENT + rank_in
    select = (
        (jnp.where(owner == a, row, -1))[None, :] == jnp.arange(160, dtype=jnp.int32)[:, None]
    ).astype(BF).reshape(2, SEGMENT, 1024)
    relative = ((owner % 4 - z) % 4) * 4 + (owner // 4 - y) % 4
    pick = (
        (relative * 160 + row)[:, None] == jnp.arange(2560, dtype=jnp.int32)[None, :]
    ).astype(BF)
    mask = (slot[:, None] == (jnp.arange(2048, dtype=jnp.int32) // 64)[None, :]).astype(BF)

    def column(r, core):
        at = ((x + r) % 4 * 2 + core) * 1024
        return lax.dynamic_slice(down_matrix, (0, at), (units, 1024))

    turns = (1, 2, 3, 0)
    empty = jnp.zeros((units, 128), BF)
    mine = jnp.concatenate([column(r, c) for r in turns] + [empty], axis=1)
    theirs = jnp.concatenate([column(r, 1 - c) for r in turns] + [empty], axis=1)

    low_own = low_own_rows(every, adapter_entry_maps, select).reshape(160, 128)
    low = jnp.stack([low_own] + [send(low_own, dy=-d) for d in (1, 2, 3)])
    low = jnp.stack([low] + [send(low, dz=-d) for d in (1, 2, 3)]).reshape(2560, 128)
    gate, up = gate_up(every, gate_matrix.T, up_matrix.T)

    exit_in, _ = lax.optimization_barrier((adapter_down_exit, low_own))
    exits = lax.all_gather(exit_in, "adapter", axis=0, tiled=True).reshape(2048, 1024)

    quarter = jnp.arange(4, dtype=jnp.int32)
    place = jnp.concatenate([way * (y - quarter) % 4, way * (z - quarter) % 4])
    rows = hidden_rows(
        place,
        gate,
        up,
        pick,
        mask,
        low,
        adapter_gate_exit.reshape(2048, units),
        adapter_up_exit.reshape(2048, units),
        adapter_down_entry.transpose(0, 2, 1).reshape(2048, units),
    )
    first_other = send(part(*rows, theirs, None, 1, 1, True, BF), dc=1)
    rest_other = send(part(*rows, theirs, None, 2, 3, True, BF), dc=1)
    first = part(*rows, mine, first_other, 1, 1, False, BF)
    rest = part(*rows, mine, rest_other, 2, 3, False, F32)

    axes = (("z", "y"), ("y", "z"))
    spans = ((0, 2048), (2048, WIDE))
    state = {}
    for step in range(3):
        for ch, (lo, hi) in enumerate(spans):
            for color in range(2):
                held = first[0, color, :, lo:hi] if step == 0 else state[ch, color]
                came = ring(held, axes[color][0]).astype(F32)
                own = rest[step, color, :, lo:hi]
                if step < 2:
                    state[ch, color] = (own + came).astype(BF)
                else:
                    state[ch, color] = (own.reshape(4, 32, -1), came.reshape(4, 32, -1))
    for ch in range(2):
        for color in range(2):
            own, came = state[ch, color]
            running = own[1] + came[1]
            for r in (2, 3, 0):
                running = own[r] + came[r] + ring(running.astype(BF), axes[color][1]).astype(F32)
            state[ch, color] = running
    summed = [jnp.concatenate([state[ch, 0], state[ch, 1]]) for ch in range(2)]
    tail = summed[1][:, 2048:]
    blocks = {
        1: summed[0][:, :1024],
        2: summed[0][:, 1024:],
        3: summed[1][:, :1024],
        0: summed[1][:, 1024:2048],
    }
    total = jnp.concatenate([blocks[0], tail], axis=1)
    for r in (1, 2, 3):
        total = total + send(
            jnp.concatenate([blocks[r], tail], axis=1).astype(BF), dx=r
        ).astype(F32)

    own_slot = jnp.sum(
        jnp.where(token_adapter[:, None] == names[None, :], adapter_slot_table[None, :], 0), axis=1
    )
    low_down = total[:, 1024:].astype(BF)
    spread = jnp.tile(low_down, (1, 16))
    spread = jnp.where(
        (own_slot // 2)[:, None] == (jnp.arange(2048, dtype=jnp.int32) // 128)[None, :], spread, 0
    )
    delta = jnp.dot(spread, exits, preferred_element_type=F32)
    return (total[:, :1024] + delta).astype(BF)


def solution(mesh):
    return jax.shard_map(
        on_device,
        mesh=mesh,
        in_specs=(
            P("adapter", "tensor"),
            P("adapter"),
            P(),
            P(None, ("adapter", "tensor")),
            P(None, ("adapter", "tensor")),
            P(("adapter", "tensor"), None),
            P("adapter", None, None),
            P(None, None, ("adapter", "tensor")),
            P(None, None, ("adapter", "tensor")),
            P(None, ("adapter", "tensor"), None),
            P("adapter", None, "tensor"),
        ),
        out_specs=P("adapter", "tensor"),
        check_vma=False,
    )
```

time: 302 us -> 313 us (1.036)
  waiting for transfers between devices: 78.8 us -> 125 us
  local copies, waits for them, and re-layouts: 40.3 us -> 10.7 us
  Pallas kernels: 84.5 us -> 67 us
  other arithmetic: 15.8 us -> 33.2 us
  matrix products: 11.3 us -> 4.23 us
    ppermute x24, waiting for transfers between devices: 16.9 us -> 53.6 us  [ring(): return lax.ppermute(value, AXES, pairs(move))]
    pallas_call x18 -> x6, Pallas kernels: 73.6 us -> 55.8 us  [the longest x4 31.6 us: part(): pl.pallas_call(functools.partial(part_kernel, turned if back else straigh...]
    convert_element_type x8 -> x20, other arithmetic: 3 us -> 20.3 us  [the longest x10 9.99 us: on_device(): running.astype(BF)]
    unnamed x55 -> x19, local copies, waits for them, and re-layouts: 24.7 us -> 7.48 us
    slice x12 -> x0, local copies, waits for them, and re-layouts: 10.1 us -> none  [the longest x4 5.43 us: on_device(): running = held[1]]
    ppermute x14 -> x11, waiting for transfers between devices: 7.46 us -> 17 us  [send(): lax.ppermute(value, AXES, pairs(lambda y, z, x, c: (y + dy, z + dz, x + d...]
    dot_general x4 -> x0, matrix products: 7.03 us -> none  [on_device(): product = jnp.dot(rows, theirs, preferred_element_type=F32).astype(BF)]
    ppermute x14 -> x11, starting transfers between devices: 15.2 us -> 15.9 us  [send(): lax.ppermute(value, AXES, pairs(lambda y, z, x, c: (y + dy, z + dz, x + d...]
  transfers between devices with their start and end apart: 40 -> 37, of which waited for: 15 -> 19; matrix products, arithmetic and copies ran while one was open for 16% -> 13% of each run, Pallas kernels for 20% -> 12%
where the time goes in v2:
time: 313 us; the launch traced here: 311 us
  waiting for transfers between devices  125 us (40%)
  Pallas kernels  67 us (21%)
  starting transfers between devices  38.9 us (12%)
  other arithmetic  33.2 us (11%)
  blocking collectives  17.5 us (6%)
  between operations  14.6 us (5%)
  local copies, waits for them, and re-layouts  10.7 us (3%)
  matrix products  4.23 us (1%)
    all_gather x1, waiting for transfers between devices, on_device(): lax.all_gather(tokens, AXES, axis=0, tiled=False).reshape(16, 8, 64, 1024)  53.9 us
    ppermute x24, waiting for transfers between devices, ring(): return lax.ppermute(value, AXES, pairs(move))  53.6 us
    pallas_call x4, Pallas kernels, part(): pl.pallas_call(functools.partial(part_kernel, turned if back else straigh...  31.6 us
    ppermute x24, starting transfers between devices, ring(): return lax.ppermute(value, AXES, pairs(move))  22.9 us
    unnamed x1, blocking collectives  17.5 us
    ppermute x11, waiting for transfers between devices, send(): lax.ppermute(value, AXES, pairs(lambda y, z, x, c: (y + dy, z + dz, x + d...  17 us
    ppermute x11, starting transfers between devices, send(): lax.ppermute(value, AXES, pairs(lambda y, z, x, c: (y + dy, z + dz, x + d...  15.9 us
    pallas_call x1, Pallas kernels, gate_up(): pl.pallas_call(gate_up_kernel, grid=(4,), in_specs=[pl.BlockSpec((16, 2,...  14 us
  transfers between devices with their start and end apart: 37, of which 19 were waited for; matrix products, arithmetic and copies ran while one was open for 13% of the time, Pallas kernels for 12%

profile of v2, /device:TPU:0, one launch (start us, length us, event | category | flops | bytes accessed | tf_op | source)
XLA Modules:
  0.0 311.4 jit_solution(3232658064844324505)
XLA Ops:
  10.3 17.5 %all-reduce = s32[1024]{0:T(1024)S(1)} all-reduce(s32[1024]{0:T(1024)S(1)} %dynamic-update-slice), channel_id=1, replica_groups=mesh['adapter'=16,'tensor'=8] {'adapter'}, use_global_device_ids=true, to_apply=%add | all-reduce | flops 1024 | bytes 8192
  33.4 2.8 compare_convert_fusion.m_ref
  36.1 3.2 %fusion.q_ref = bf16[1024,2560]{1,0:T(8,128)(2,1)} fusion(s32[1024]{0:T(1024)S(1)} %get-tuple-element.48), kind=kLoop, calls=%fused_computation.1 | loop fusion | flops 5242880 | bytes 5246976 | tf_op jit(solution)/shard_map/convert_element_type | solution.py:284
  39.4 53.9 %all-gather.6.cloned.1.call-done = bf16[8192,1024]{1,0:T(8,128)(2,1)} async-done(((bf16[64,1024]{1,0:T(8,128)(2,1)}), bf16[8192,1024]{1,0:T(8,128)(2,1)}) %all-gather.6.cloned.1.call-update) | async-done | bytes 16777232 | tf_op jit(solution)/shard_map/all_gather | solution.py:266
  93.3 10.2 %low_own.1 = bf16[2,80,128]{2,1,0:T(8,128)(2,1)} custom-call(bf16[16,8,64,1024]{3,2,1,0:T(8,128)(2,1)} %bitcast.148, bf16[2,8192,128]{2,1,0:T(8,128)(2,1)} %e_ref.1, bf16[2,80,1024]{2,1,0:T(8,128)(2,1)} %compare_convert_fusion.1.s_ref), custom_call_target="tpu_custom_call" | custom-call | flops 4294967296 | bytes 22020096 | tf_op jit(solution)/shard_map/low_own/pallas_call | solution.py:70
  105.0 2.7 collective-permute-start.1
  113.9 2.9 collective-permute-start.4
  118.1 14.0 %gate_up.1 = (f32[1024,224]{1,0:T(8,128)}, f32[1024,224]{1,0:T(8,128)}) custom-call(bf16[16,8,64,1024]{3,2,1,0:T(8,128)(2,1)} %bitcast.149, bf16[224,8192]{1,0:T(8,128)(2,1)} %bitcast.166, bf16[224,8192]{1,0:T(8,128)(2,1)} %bitcast.167), custom_call_target="tpu_custom_call" | custom-call | flops 8589934592 | bytes 26214400 | tf_op jit(solution)/shard_map/gate_up/pallas_call | solution.py:106
  133.1 11.2 %hidden_rows.1 = (bf16[4,4,32,224]{3,2,1,0:T(8,128)(2,1)}, bf16[4,4,32,224]{3,2,1,0:T(8,128)(2,1)}, f32[4,4,32,128]{3,2,1,0:T(8,128)}, f32[4,4,32,128]{3,2,1,0:T(8,128)}) custom-call(s32[8]{0:T(128)} %pad_add_fusion.place, f32[1024,224]{1,0:T(8,128)} %get-tuple-element.12.g_ref, f32[1024,224]{1,0:T(8,128)} %get-tuple-element.13.u_ref, ...), custom_call_target="tpu_custom_call" | custom-call | flops 2684354560 | bytes 16777216 | tf_op jit(solution)/shard_map/hidden_rows/pallas_call | solution.py:154
  144.3 9.2 %part.4 = bf16[3,2,128,4224]{3,2,1,0:T(8,128)(2,1)} custom-call(bf16[4,4,32,224]{3,2,1,0:T(8,128)(2,1)} %get-tuple-element.14.ha_ref, bf16[4,4,32,224]{3,2,1,0:T(8,128)(2,1)} %get-tuple-element.15.hb_ref, f32[4,4,32,128]{3,2,1,0:T(8,128)} %get-tuple-element.16.da_ref, f32[4,4,32,128]{3,2,1,0:T(8,128)} %get-tuple-element.17.db_ref, bf16[224,4224]{1,0:T(8,128)(2,1)} %copy-done), custom_call_target="tpu_custom_call" | custom-call | flops 1660944384 | bytes 21356544 | tf_op jit(solution)/shard_map/part/pallas_call | solution.py:231
  153.5 4.3 %part.6 = bf16[1,2,128,4224]{3,2,1,0:T(8,128)(2,1)} custom-call(bf16[4,4,32,224]{3,2,1,0:T(8,128)(2,1)} %get-tuple-element.14.ha_ref, bf16[4,4,32,224]{3,2,1,0:T(8,128)(2,1)} %get-tuple-element.15.hb_ref, f32[4,4,32,128]{3,2,1,0:T(8,128)} %get-tuple-element.16.da_ref, f32[4,4,32,128]{3,2,1,0:T(8,128)} %get-tuple-element.17.db_ref, bf16[224,4224]{1,0:T(8,128)(2,1)} %copy-done), custom_call_target="tpu_custom_call" | custom-call | flops 553648128 | bytes 8380416 | tf_op jit(solution)/shard_map/part/pallas_call | solution.py:231
  158.9 8.3 %collective-permute-done.7.refs_0_ = bf16[1,2,128,4224]{3,2,1,0:T(8,128)(2,1)S(1)} collective-permute-done((bf16[1,2,128,4224]{3,2,1,0:T(8,128)(2,1)}, bf16[1,2,128,4224]{3,2,1,0:T(8,128)(2,1)S(1)}, u32[]{:S(2)}, u32[]{:S(2)}) %collective-permute-start.7) | collective-permute-done | bytes 2162720 | tf_op jit(solution)/shard_map/ppermute | solution.py:27
  168.6 4.8 %part.7 = bf16[1,2,128,4224]{3,2,1,0:T(8,128)(2,1)} custom-call(bf16[4,4,32,224]{3,2,1,0:T(8,128)(2,1)} %get-tuple-element.14.ha_ref, bf16[4,4,32,224]{3,2,1,0:T(8,128)(2,1)} %get-tuple-element.15.hb_ref, f32[4,4,32,128]{3,2,1,0:T(8,128)} %get-tuple-element.16.da_ref, f32[4,4,32,128]{3,2,1,0:T(8,128)} %get-tuple-element.17.db_ref, ...), custom_call_target="tpu_custom_call" | custom-call | flops 553648128 | bytes 8380416 | tf_op jit(solution)/shard_map/part/pallas_call | solution.py:231
  178.6 13.3 %part.5 = f32[3,2,128,4224]{3,2,1,0:T(8,128)} custom-call(bf16[4,4,32,224]{3,2,1,0:T(8,128)(2,1)} %get-tuple-element.14.ha_ref, bf16[4,4,32,224]{3,2,1,0:T(8,128)(2,1)} %get-tuple-element.15.hb_ref, f32[4,4,32,128]{3,2,1,0:T(8,128)} %get-tuple-element.16.da_ref, f32[4,4,32,128]{3,2,1,0:T(8,128)} %get-tuple-element.17.db_ref, ...), custom_call_target="tpu_custom_call" | custom-call | flops 1660944384 | bytes 21356544 | tf_op jit(solution)/shard_map/part/pallas_call | solution.py:231
  191.9 2.2 fusion.18
  196.0 2.7 collective-permute-start.15
  198.8 5.8 %collective-permute-done.21 = bf16[128,2048]{1,0:T(8,128)(2,1)S(1)} collective-permute-done((bf16[128,2048]{1,0:T(8,128)(2,1)}, bf16[128,2048]{1,0:T(8,128)(2,1)S(1)}, u32[]{:S(2)}, u32[]{:S(2)}) %collective-permute-start.21) | collective-permute-done | bytes 524320 | tf_op jit(solution)/shard_map/ppermute | solution.py:35
  204.7 2.0 fusion.20
  207.0 2.6 collective-permute-start.27
  211.4 2.4 collective-permute-start.9
  214.4 5.9 %collective-permute-done.22 = bf16[128,2048]{1,0:T(8,128)(2,1)S(1)} collective-permute-done((bf16[128,2048]{1,0:T(8,128)(2,1)S(1)}, bf16[128,2048]{1,0:T(8,128)(2,1)S(1)}, u32[]{:S(2)}, u32[]{:S(2)}) %collective-permute-start.22) | collective-permute-done | bytes 524320 | tf_op jit(solution)/shard_map/ppermute | solution.py:35
  221.3 3.0 collective-permute-start.23
  233.1 4.7 %collective-permute-done.17 = bf16[32,2176]{1,0:T(8,128)(2,1)S(1)} collective-permute-done((bf16[32,2176]{1,0:T(8,128)(2,1)S(1)}, bf16[32,2176]{1,0:T(8,128)(2,1)S(1)}, u32[]{:S(2)}, u32[]{:S(2)}) %collective-permute-start.17) | collective-permute-done | bytes 139296 | tf_op jit(solution)/shard_map/ppermute | solution.py:35
  240.8 18.4 %collective-permute-done.18 = bf16[32,2176]{1,0:T(8,128)(2,1)S(1)} collective-permute-done((bf16[32,2176]{1,0:T(8,128)(2,1)S(1)}, bf16[32,2176]{1,0:T(8,128)(2,1)S(1)}, u32[]{:S(2)}, u32[]{:S(2)}) %collective-permute-start.18) | collective-permute-done | bytes 139296 | tf_op jit(solution)/shard_map/ppermute | solution.py:35
  263.5 3.0 collective-permute-done.19
  269.4 4.5 %collective-permute-done.11 = bf16[32,2176]{1,0:T(8,128)(2,1)S(1)} collective-permute-done((bf16[32,2176]{1,0:T(8,128)(2,1)S(1)}, bf16[32,2176]{1,0:T(8,128)(2,1)S(1)}, u32[]{:S(2)}, u32[]{:S(2)}) %collective-permute-start.11) | collective-permute-done | bytes 139296 | tf_op jit(solution)/shard_map/ppermute | solution.py:35
  276.6 4.7 %collective-permute-done.12 = bf16[32,2176]{1,0:T(8,128)(2,1)S(1)} collective-permute-done((bf16[32,2176]{1,0:T(8,128)(2,1)S(1)}, bf16[32,2176]{1,0:T(8,128)(2,1)S(1)}, u32[]{:S(2)}, u32[]{:S(2)}) %collective-permute-start.12) | collective-permute-done | bytes 139296 | tf_op jit(solution)/shard_map/ppermute | solution.py:35
  283.9 4.7 %collective-permute-done.13 = bf16[32,2176]{1,0:T(8,128)(2,1)S(1)} collective-permute-done((bf16[32,2176]{1,0:T(8,128)(2,1)S(1)}, bf16[32,2176]{1,0:T(8,128)(2,1)S(1)}, u32[]{:S(2)}, u32[]{:S(2)}) %collective-permute-start.13) | collective-permute-done | bytes 139296 | tf_op jit(solution)/shard_map/ppermute | solution.py:35
  289.7 2.7 collective-permute-start.34
  294.1 2.6 collective-permute-done.34
  296.6 2.5 collective-permute-done.33
  300.8 3.7 %fusion.40 = bf16[64,1024]{1,0:T(8,128)(2,1)} fusion(f32[64,1152]{1,0:T(8,128)S(1)} %fusion.24, bf16[2048,1024]{1,0:T(8,128)(2,1)} %bitcast.150, bf16[8,8,16,128]{3,2,1,0:T(8,128)(2,1)S(1)} %bitcast.155), kind=kOutput, calls=%fused_computation.88 | convolution fusion | flops 268566528 | bytes 4849664 | tf_op jit(solution)/shard_map/dot_general | solution.py:364
  (122 shorter events, 60.4 us)
Async XLA Ops:
  6.5 86.8 %all-gather.6.cloned.1.call-start = ((), (), s32[]{:S(2)}) async-start(), calls=%async_computation.1 | async-start | bytes 16908288 | tf_op jit(solution)/shard_map/all_gather | solution.py:266
  7.3 293.6 %all-gather.4.cloned.1.call-start = ((), (), s32[]{:S(2)}) async-start(), calls=%async_computation | async-start | bytes 4456448 | tf_op jit(solution)/shard_map/all_gather | solution.py:302
  112.7 19.4 %collective-permute-start.5 = (bf16[4,160,128]{2,1,0:T(8,128)(2,1)S(1)}, bf16[4,160,128]{2,1,0:T(8,128)(2,1)S(1)}, u32[]{:S(2)}, u32[]{:S(2)}) collective-permute-start(bf16[4,160,128]{2,1,0:T(8,128)(2,1)S(1)} %get-tuple-element.44), channel_id=1, source_target_pairs={{0,8},{1,9},{2,10},{3,11},{4,12},{5,13},{6,14},{7,15},{8,16},{9,17... | collective-permute-start | bytes 491528 | tf_op jit(solution)/shard_map/ppermute | solution.py:27
  113.9 18.3 %collective-permute-start.4 = (bf16[4,160,128]{2,1,0:T(8,128)(2,1)S(1)}, bf16[4,160,128]{2,1,0:T(8,128)(2,1)S(1)}, u32[]{:S(2)}, u32[]{:S(2)}) collective-permute-start(bf16[4,160,128]{2,1,0:T(8,128)(2,1)S(1)} %get-tuple-element.44), channel_id=1, source_target_pairs={{0,16},{1,17},{2,18},{3,19},{4,20},{5,21},{6,22},{7,23},{8,24},{9,... | collective-permute-start | bytes 491528 | tf_op jit(solution)/shard_map/ppermute | solution.py:27
  116.7 15.4 %collective-permute-start.3 = (bf16[4,160,128]{2,1,0:T(8,128)(2,1)S(1)}, bf16[4,160,128]{2,1,0:T(8,128)(2,1)S(1)}, u32[]{:S(2)}, u32[]{:S(2)}) collective-permute-start(bf16[4,160,128]{2,1,0:T(8,128)(2,1)S(1)} %get-tuple-element.44), channel_id=1, source_target_pairs={{0,24},{1,25},{2,26},{3,27},{4,28},{5,29},{6,30},{7,31},{8,0},{9,1... | collective-permute-start | bytes 491528 | tf_op jit(solution)/shard_map/ppermute | solution.py:27
  153.5 25.1 %collective-permute-start.6 = (bf16[3,2,128,4224]{3,2,1,0:T(8,128)(2,1)}, bf16[3,2,128,4224]{3,2,1,0:T(8,128)(2,1)}, u32[]{:S(2)}, u32[]{:S(2)}) collective-permute-start(bf16[3,2,128,4224]{3,2,1,0:T(8,128)(2,1)} %part.4), channel_id=1, source_target_pairs={{0,1},{1,0},{2,3},{3,2},{4,5},{5,4},{6,7},{7,6},{8,9},{9,8},{10,11... | collective-permute-start | bytes 19464200 | tf_op jit(solution)/shard_map/ppermute | solution.py:27
  157.7 9.5 %collective-permute-start.7 = (bf16[1,2,128,4224]{3,2,1,0:T(8,128)(2,1)}, bf16[1,2,128,4224]{3,2,1,0:T(8,128)(2,1)S(1)}, u32[]{:S(2)}, u32[]{:S(2)}) collective-permute-start(bf16[1,2,128,4224]{3,2,1,0:T(8,128)(2,1)} %part.6), channel_id=1, source_target_pairs={{0,1},{1,0},{2,3},{3,2},{4,5},{5,4},{6,7},{7,6},{8,9},{9,8},{10,11... | collective-permute-start | bytes 6488072 | tf_op jit(solution)/shard_map/ppermute | solution.py:27
  174.7 17.2 %collective-permute-start.20 = (bf16[128,2048]{1,0:T(8,128)(2,1)S(1)}, bf16[128,2048]{1,0:T(8,128)(2,1)S(1)}, u32[]{:S(2)}, u32[]{:S(2)}) collective-permute-start(bf16[128,2048]{1,0:T(8,128)(2,1)S(1)} %get-tuple-element.37), channel_id=1, source_target_pairs={{0,8},{1,25},{2,10},{3,27},{4,12},{5,29},{6,14},{7,31},{8,16},{9,1... | collective-permute-start | bytes 1572872 | tf_op jit(solution)/shard_map/ppermute | solution.py:35
  176.8 17.8 %collective-permute-start.14 = (bf16[128,2176]{1,0:T(8,128)(2,1)S(1)}, bf16[128,2176]{1,0:T(8,128)(2,1)S(1)}, u32[]{:S(2)}, u32[]{:S(2)}) collective-permute-start(bf16[128,2176]{1,0:T(8,128)(2,1)S(1)} %get-tuple-element.39), channel_id=1, source_target_pairs={{0,32},{1,97},{2,34},{3,99},{4,36},{5,101},{6,38},{7,103},{8,40},{... | collective-permute-start | bytes 1671176 | tf_op jit(solution)/shard_map/ppermute | solution.py:35
  177.3 32.3 %collective-permute-start.8 = (bf16[128,2176]{1,0:T(8,128)(2,1)S(1)}, bf16[128,2176]{1,0:T(8,128)(2,1)S(1)}, u32[]{:S(2)}, u32[]{:S(2)}) collective-permute-start(bf16[128,2176]{1,0:T(8,128)(2,1)S(1)} %get-tuple-element.40), channel_id=1, source_target_pairs={{0,8},{1,25},{2,10},{3,27},{4,12},{5,29},{6,14},{7,31},{8,16},{9,1... | collective-permute-start | bytes 1671176 | tf_op jit(solution)/shard_map/ppermute | solution.py:35
  177.5 21.4 %collective-permute-start.26 = (bf16[128,2048]{1,0:T(8,128)(2,1)S(1)}, bf16[128,2048]{1,0:T(8,128)(2,1)}, u32[]{:S(2)}, u32[]{:S(2)}) collective-permute-start(bf16[128,2048]{1,0:T(8,128)(2,1)S(1)} %get-tuple-element.38), channel_id=1, source_target_pairs={{0,32},{1,97},{2,34},{3,99},{4,36},{5,101},{6,38},{7,103},{8,40},{... | collective-permute-start | bytes 1572872 | tf_op jit(solution)/shard_map/ppermute | solution.py:35
  194.1 10.6 %collective-permute-start.21 = (bf16[128,2048]{1,0:T(8,128)(2,1)}, bf16[128,2048]{1,0:T(8,128)(2,1)S(1)}, u32[]{:S(2)}, u32[]{:S(2)}) collective-permute-start(bf16[128,2048]{1,0:T(8,128)(2,1)} %fusion.18), channel_id=1, source_target_pairs={{0,8},{1,25},{2,10},{3,27},{4,12},{5,29},{6,14},{7,31},{8,16},{9,1... | collective-permute-start | bytes 1572872 | tf_op jit(solution)/shard_map/ppermute | solution.py:35
  196.0 13.6 %collective-permute-start.15 = (bf16[128,2176]{1,0:T(8,128)(2,1)S(1)}, bf16[128,2176]{1,0:T(8,128)(2,1)S(1)}, u32[]{:S(2)}, u32[]{:S(2)}) collective-permute-start(bf16[128,2176]{1,0:T(8,128)(2,1)S(1)} %fusion.6), channel_id=1, source_target_pairs={{0,32},{1,97},{2,34},{3,99},{4,36},{5,101},{6,38},{7,103},{8,40},{... | collective-permute-start | bytes 1671176 | tf_op jit(solution)/shard_map/ppermute | solution.py:35
  206.6 13.6 %collective-permute-start.22 = (bf16[128,2048]{1,0:T(8,128)(2,1)S(1)}, bf16[128,2048]{1,0:T(8,128)(2,1)S(1)}, u32[]{:S(2)}, u32[]{:S(2)}) collective-permute-start(bf16[128,2048]{1,0:T(8,128)(2,1)S(1)} %get-tuple-element.23), channel_id=1, source_target_pairs={{0,8},{1,25},{2,10},{3,27},{4,12},{5,29},{6,14},{7,31},{8,16},{9,1... | collective-permute-start | bytes 1572872 | tf_op jit(solution)/shard_map/ppermute | solution.py:35
  207.0 17.4 %collective-permute-start.27 = (bf16[128,2048]{1,0:T(8,128)(2,1)S(1)}, bf16[128,2048]{1,0:T(8,128)(2,1)S(1)}, u32[]{:S(2)}, u32[]{:S(2)}) collective-permute-start(bf16[128,2048]{1,0:T(8,128)(2,1)S(1)} %get-tuple-element.24), channel_id=1, source_target_pairs={{0,32},{1,97},{2,34},{3,99},{4,36},{5,101},{6,38},{7,103},{8,40},{... | collective-permute-start | bytes 1572872 | tf_op jit(solution)/shard_map/ppermute | solution.py:35
  211.4 18.9 %collective-permute-start.9 = (bf16[128,2176]{1,0:T(8,128)(2,1)S(1)}, bf16[128,2176]{1,0:T(8,128)(2,1)S(1)}, u32[]{:S(2)}, u32[]{:S(2)}) collective-permute-start(bf16[128,2176]{1,0:T(8,128)(2,1)S(1)} %get-tuple-element.28), channel_id=1, source_target_pairs={{0,8},{1,25},{2,10},{3,27},{4,12},{5,29},{6,14},{7,31},{8,16},{9,1... | collective-permute-start | bytes 1671176 | tf_op jit(solution)/shard_map/ppermute | solution.py:35
  213.8 13.7 %collective-permute-start.16 = (bf16[128,2176]{1,0:T(8,128)(2,1)S(1)}, bf16[128,2176]{1,0:T(8,128)(2,1)S(1)}, u32[]{:S(2)}, u32[]{:S(2)}) collective-permute-start(bf16[128,2176]{1,0:T(8,128)(2,1)S(1)} %get-tuple-element.27), channel_id=1, source_target_pairs={{0,32},{1,97},{2,34},{3,99},{4,36},{5,101},{6,38},{7,103},{8,40},{... | collective-permute-start | bytes 1671176 | tf_op jit(solution)/shard_map/ppermute | solution.py:35
  221.3 17.8 %collective-permute-start.23 = (bf16[32,2048]{1,0:T(8,128)(2,1)S(1)}, bf16[32,2048]{1,0:T(8,128)(2,1)S(1)}, u32[]{:S(2)}, u32[]{:S(2)}) collective-permute-start(bf16[32,2048]{1,0:T(8,128)(2,1)S(1)} %fusion.48), channel_id=1, source_target_pairs={{0,32},{1,97},{2,34},{3,99},{4,36},{5,101},{6,38},{7,103},{8,40},{... | collective-permute-start | bytes 393224 | tf_op jit(solution)/shard_map/ppermute | solution.py:35
  225.7 34.6 %collective-permute-start.28 = (bf16[128,2048]{1,0:T(8,128)(2,1)S(1)}, bf16[128,2048]{1,0:T(8,128)(2,1)S(1)}, u32[]{:S(2)}, u32[]{:S(2)}) collective-permute-start(bf16[128,2048]{1,0:T(8,128)(2,1)S(1)} %fusion.16), channel_id=1, source_target_pairs={{0,32},{1,97},{2,34},{3,99},{4,36},{5,101},{6,38},{7,103},{8,40},{... | collective-permute-start | bytes 1572872 | tf_op jit(solution)/shard_map/ppermute | solution.py:35
  228.6 9.3 %collective-permute-start.17 = (bf16[32,2176]{1,0:T(8,128)(2,1)S(1)}, bf16[32,2176]{1,0:T(8,128)(2,1)S(1)}, u32[]{:S(2)}, u32[]{:S(2)}) collective-permute-start(bf16[32,2176]{1,0:T(8,128)(2,1)S(1)} %fusion.25), channel_id=1, source_target_pairs={{0,8},{1,25},{2,10},{3,27},{4,12},{5,29},{6,14},{7,31},{8,16},{9,1... | collective-permute-start | bytes 417800 | tf_op jit(solution)/shard_map/ppermute | solution.py:35
  231.6 31.8 %collective-permute-start.10 = (bf16[128,2176]{1,0:T(8,128)(2,1)S(1)}, bf16[128,2176]{1,0:T(8,128)(2,1)S(1)}, u32[]{:S(2)}, u32[]{:S(2)}) collective-permute-start(bf16[128,2176]{1,0:T(8,128)(2,1)S(1)} %fusion.12), channel_id=1, source_target_pairs={{0,8},{1,25},{2,10},{3,27},{4,12},{5,29},{6,14},{7,31},{8,16},{9,1... | collective-permute-start | bytes 1671176 | tf_op jit(solution)/shard_map/ppermute | solution.py:35
  238.8 20.4 %collective-permute-start.18 = (bf16[32,2176]{1,0:T(8,128)(2,1)S(1)}, bf16[32,2176]{1,0:T(8,128)(2,1)S(1)}, u32[]{:S(2)}, u32[]{:S(2)}) collective-permute-start(bf16[32,2176]{1,0:T(8,128)(2,1)S(1)} %fusion.27), channel_id=1, source_target_pairs={{0,8},{1,25},{2,10},{3,27},{4,12},{5,29},{6,14},{7,31},{8,16},{9,1... | collective-permute-start | bytes 417800 | tf_op jit(solution)/shard_map/ppermute | solution.py:35
  240.1 20.3 %collective-permute-start.24 = (bf16[32,2048]{1,0:T(8,128)(2,1)S(1)}, bf16[32,2048]{1,0:T(8,128)(2,1)S(1)}, u32[]{:S(2)}, u32[]{:S(2)}) collective-permute-start(bf16[32,2048]{1,0:T(8,128)(2,1)S(1)} %fusion.50), channel_id=1, source_target_pairs={{0,32},{1,97},{2,34},{3,99},{4,36},{5,101},{6,38},{7,103},{8,40},{... | collective-permute-start | bytes 393224 | tf_op jit(solution)/shard_map/ppermute | solution.py:35
  260.2 6.3 %collective-permute-start.19 = (bf16[32,2176]{1,0:T(8,128)(2,1)S(1)}, bf16[32,2176]{1,0:T(8,128)(2,1)S(1)}, u32[]{:S(2)}, u32[]{:S(2)}) collective-permute-start(bf16[32,2176]{1,0:T(8,128)(2,1)S(1)} %fusion.29), channel_id=1, source_target_pairs={{0,8},{1,25},{2,10},{3,27},{4,12},{5,29},{6,14},{7,31},{8,16},{9,1... | collective-permute-start | bytes 417800 | tf_op jit(solution)/shard_map/ppermute | solution.py:35
  261.5 20.9 %collective-permute-start.25 = (bf16[32,2048]{1,0:T(8,128)(2,1)S(1)}, bf16[32,2048]{1,0:T(8,128)(2,1)S(1)}, u32[]{:S(2)}, u32[]{:S(2)}) collective-permute-start(bf16[32,2048]{1,0:T(8,128)(2,1)S(1)} %get-tuple-element.21), channel_id=1, source_target_pairs={{0,32},{1,97},{2,34},{3,99},{4,36},{5,101},{6,38},{7,103},{8,40},{... | collective-permute-start | bytes 393224 | tf_op jit(solution)/shard_map/ppermute | solution.py:35
  267.6 6.3 %collective-permute-start.11 = (bf16[32,2176]{1,0:T(8,128)(2,1)S(1)}, bf16[32,2176]{1,0:T(8,128)(2,1)S(1)}, u32[]{:S(2)}, u32[]{:S(2)}) collective-permute-start(bf16[32,2176]{1,0:T(8,128)(2,1)S(1)} %get-tuple-element.26), channel_id=1, source_target_pairs={{0,32},{1,97},{2,34},{3,99},{4,36},{5,101},{6,38},{7,103},{8,40},{... | collective-permute-start | bytes 417800 | tf_op jit(solution)/shard_map/ppermute | solution.py:35
  269.3 6.2 %collective-permute-start.30 = (bf16[32,2048]{1,0:T(8,128)(2,1)S(1)}, bf16[32,2048]{1,0:T(8,128)(2,1)S(1)}, u32[]{:S(2)}, u32[]{:S(2)}) collective-permute-start(bf16[32,2048]{1,0:T(8,128)(2,1)S(1)} %fusion.44), channel_id=1, source_target_pairs={{0,8},{1,25},{2,10},{3,27},{4,12},{5,29},{6,14},{7,31},{8,16},{9,1... | collective-permute-start | bytes 393224 | tf_op jit(solution)/shard_map/ppermute | solution.py:35
  275.0 6.3 %collective-permute-start.12 = (bf16[32,2176]{1,0:T(8,128)(2,1)S(1)}, bf16[32,2176]{1,0:T(8,128)(2,1)S(1)}, u32[]{:S(2)}, u32[]{:S(2)}) collective-permute-start(bf16[32,2176]{1,0:T(8,128)(2,1)S(1)} %fusion.33), channel_id=1, source_target_pairs={{0,32},{1,97},{2,34},{3,99},{4,36},{5,101},{6,38},{7,103},{8,40},{... | collective-permute-start | bytes 417800 | tf_op jit(solution)/shard_map/ppermute | solution.py:35
  282.3 6.3 %collective-permute-start.13 = (bf16[32,2176]{1,0:T(8,128)(2,1)S(1)}, bf16[32,2176]{1,0:T(8,128)(2,1)S(1)}, u32[]{:S(2)}, u32[]{:S(2)}) collective-permute-start(bf16[32,2176]{1,0:T(8,128)(2,1)S(1)} %fusion.35), channel_id=1, source_target_pairs={{0,32},{1,97},{2,34},{3,99},{4,36},{5,101},{6,38},{7,103},{8,40},{... | collective-permute-start | bytes 417800 | tf_op jit(solution)/shard_map/ppermute | solution.py:35
  289.7 6.9 %collective-permute-start.34 = (bf16[64,1152]{1,0:T(8,128)(2,1)S(1)}, bf16[64,1152]{1,0:T(8,128)(2,1)S(1)}, u32[]{:S(2)}, u32[]{:S(2)}) collective-permute-start(bf16[64,1152]{1,0:T(8,128)(2,1)S(1)} %get-tuple-element.47), channel_id=1, source_target_pairs={{0,6},{1,7},{2,0},{3,1},{4,2},{5,3},{6,4},{7,5},{8,14},{9,15},{10,... | collective-permute-start | bytes 442376 | tf_op jit(solution)/shard_map/ppermute | solution.py:27
  292.4 6.8 %collective-permute-start.33 = (bf16[64,1152]{1,0:T(8,128)(2,1)S(1)}, bf16[64,1152]{1,0:T(8,128)(2,1)S(1)}, u32[]{:S(2)}, u32[]{:S(2)}) collective-permute-start(bf16[64,1152]{1,0:T(8,128)(2,1)S(1)} %get-tuple-element.46), channel_id=1, source_target_pairs={{0,4},{1,5},{2,6},{3,7},{4,0},{5,1},{6,2},{7,3},{8,12},{9,13},{10,... | collective-permute-start | bytes 442376 | tf_op jit(solution)/shard_map/ppermute | solution.py:27
  293.2 7.4 %collective-permute-start.32 = (bf16[64,1152]{1,0:T(8,128)(2,1)S(1)}, bf16[64,1152]{1,0:T(8,128)(2,1)S(1)}, u32[]{:S(2)}, u32[]{:S(2)}) collective-permute-start(bf16[64,1152]{1,0:T(8,128)(2,1)S(1)} %get-tuple-element.45), channel_id=1, source_target_pairs={{0,2},{1,3},{2,4},{3,5},{4,6},{5,7},{6,0},{7,1},{8,10},{9,11},{10,... | collective-permute-start | bytes 442376 | tf_op jit(solution)/shard_map/ppermute | solution.py:27
  (11 other events, 46.5 us)
Sparse Core Ops, SparseCore 0:
  10.5 82.7 all-gather.5
  199.0 60.1 all-gather.3
